TPU v7x, 32 devices: a whole 2x2x4 slice. The times are simulated.
32 devices in a mesh: grp: 2 (over y), br: 4 (over z), rhs: 2 (over x), sub: 2 (over core).
Axes of the slice: x: 2, y: 2, z: 4, core: 2. Of those that a mesh axis runs over, the one named last changes fastest.
Arguments:
- sources: bfloat16 [64, 64, 2048], P(('grp', 'rhs', 'sub'), 'br'), parts along dimension 0, may hold values from -6 to 6
- leaf_basis: bfloat16 [64, 64, 4096], P(('grp', 'rhs', 'sub'), 'br'), parts along dimension 0, may hold values from -0.75 to 0.75
- transfer: bfloat16 [3, 4, 4096], replicated, may hold values from -0.375 to 0.375
- coupling: bfloat16 [4, 49, 4096], replicated, may hold values from -0.15625 to 0.15625
- near_table: bfloat16 [9, 4096], replicated, may hold values from -0.25 to 0.25
- near_mask: int32 [64, 64, 9], P(('grp', 'rhs', 'sub'), 'br'), parts along dimension 0, may hold values 0 or 1
- mask_leaf: int32 [64, 64, 27], P(('grp', 'rhs', 'sub'), 'br'), parts along dimension 0, may hold values 0 or 1
- mask_mid: int32 [32, 32, 27], P(('grp', 'rhs', 'sub'), 'br'), parts along dimension 0, may hold values 0 or 1
- mask_upper: int32 [16, 16, 27], P('grp', 'br'), parts along dimension 0, may hold values 0 or 1
- mask_top: int32 [8, 8, 27], P('grp', 'br'), parts along dimension 0, may hold values 0 or 1
Outputs:
- result: bfloat16 [64, 64, 2048], P(('grp', 'rhs', 'sub'), 'br'), parts along dimension 0
There are 2 independent parts, one for each index of `grp`. A program takes and returns all parts, laid end to end along the dimension named above; an argument that names none is the same for every part. Nothing has to cross between parts.
Inputs may be any that keep to these rules, and one draw needn't show every extreme that they name: `near_mask`: 1 keeps a neighbour in a leaf's near-field list, 0 marks a padded entry. `mask_leaf`: 1 keeps an entry of a node's coupling list, 0 marks a padded one. `mask_mid`: 1 keeps an entry of a node's coupling list, 0 marks a padded one. `mask_upper`: 1 keeps an entry of a node's coupling list, 0 marks a padded one. `mask_top`: 1 keeps an entry of a node's coupling list, 0 marks a padded one.
All inputs are finite; a program needn't handle non-finite values. No bound on the sum of `near_mask` or of `mask_leaf` or of `mask_mid` or of `mask_upper` or of `mask_top` on one device may be relied on, other than what follows from the above.
Results may differ from a plain program's by a relative error of at most 0.017.
Values may be sent and summed in bfloat16 or wider, within the bound.
No kernel may reach another device: no remote copies, remote signals or barrier semaphores. Data moves between devices by JAX's collectives and lax.ppermute only.
A program may use at most 192 MiB of HBM per device.

v0:
```python
import jax
import jax.numpy as jnp
from jax import lax
from jax.sharding import PartitionSpec as P

LEAF = 64
RANK = 64
SIDES = 32
PRODUCTS = 3


def with_halo(block, sides, width):
    for axis, dim in sides:
        count = lax.axis_size(axis)
        forward = [(i, i + 1) for i in range(count - 1)]
        backward = [(target, source) for source, target in forward]
        low = lax.ppermute(
            lax.slice_in_dim(block, block.shape[dim] - width, None, axis=dim), axis, forward
        )
        high = lax.ppermute(lax.slice_in_dim(block, 0, width, axis=dim), axis, backward)
        block = jnp.concatenate([low, block, high], axis=dim)
    return block


def paired(matrices):
    width = matrices.shape[-1]
    unit = jnp.eye(2, dtype=matrices.dtype)
    lead = matrices.shape[:-2]
    expanded = unit[:, None, :, None] * matrices[..., None, :, None, :]
    return expanded.reshape(lead + (2 * width, 2 * width))


def couple_block(padded, slot_mask, op_table):
    span_rows, span_cols = (padded.shape[0] - 4, padded.shape[1] - 4)
    coeffs = padded.reshape(span_rows + 4, span_cols + 4, SIDES // 2, 2 * RANK)
    matrices = paired(op_table.reshape(49, RANK, RANK))
    results = {}
    for row_par in range(2):
        for col_par in range(2):
            windows = []
            tables = []
            slot_index = 0
            for win_row in range(6):
                for win_col in range(6):
                    row_step = win_row - 2 - row_par
                    col_step = win_col - 2 - col_par
                    if abs(row_step) <= 1 and abs(col_step) <= 1:
                        continue
                    source = coeffs[
                        win_row : win_row + span_rows : 2, win_col : win_col + span_cols : 2
                    ]
                    kept_mask = slot_mask[row_par::2, col_par::2, slot_index].astype(coeffs.dtype)
                    windows.append(source * kept_mask[:, :, None, None])
                    tables.append(matrices[(row_step + 3) * 7 + col_step + 3])
                    slot_index = slot_index + 1
            stacked = jnp.concatenate(windows, 3)
            joined_table = jnp.concatenate(tables, 0)
            results[row_par, col_par] = jnp.einsum(
                "ijsr,rt->ijst", stacked, joined_table, preferred_element_type=jnp.float32
            )
    row_parts = [jnp.stack([results[row_par, 0], results[row_par, 1]], 2) for row_par in range(2)]
    total = jnp.stack(row_parts, 1)
    return total.reshape(span_rows, span_cols, SIDES * RANK)


def column_couple(column, full_mask, op_table, start, wanted):
    column = jnp.pad(column, ((2, 2), (0, 0), (0, 0)))
    span_len = wanted + wanted % 2
    lower = start - start % 2
    window = lax.dynamic_slice_in_dim(column, lower, span_len + 4, 0)
    window_mask = lax.dynamic_slice_in_dim(full_mask, lower, span_len, 0)
    coupled = couple_block(window, window_mask, op_table)
    return lax.dynamic_slice_in_dim(coupled, start % 2, wanted, 0)


def upward(child, transfer_level):
    span_rows, span_cols = (child.shape[0] // 2, child.shape[1] // 2)
    blocks = child.reshape(span_rows, 2, span_cols, 2, SIDES // 2, 2 * RANK)
    matrices = paired(transfer_level.reshape(2, 2, RANK, RANK))
    parent = jnp.einsum("iajbsr,abrt->ijst", blocks, matrices, preferred_element_type=jnp.float32)
    return parent.astype(jnp.bfloat16).reshape(span_rows, span_cols, SIDES * RANK)


def downward(parent, transfer_level):
    span_rows, span_cols = (parent.shape[0], parent.shape[1])
    rounded = parent.astype(jnp.bfloat16).reshape(span_rows, span_cols, SIDES // 2, 2 * RANK)
    matrices = paired(transfer_level.reshape(2, 2, RANK, RANK))
    child = jnp.einsum("ijst,abrt->iajbsr", rounded, matrices, preferred_element_type=jnp.float32)
    return child.reshape(2 * span_rows, 2 * span_cols, SIDES * RANK)


def near_field(field_pad, near_table, near_mask):
    span_rows, span_cols = (near_mask.shape[0], near_mask.shape[1])
    points = field_pad.reshape(span_rows + 2, span_cols + 2, SIDES // 2, 2 * LEAF)
    matrices = paired(near_table.reshape(9, LEAF, LEAF))
    windows = []
    for row_shift in range(3):
        for col_shift in range(3):
            source = points[row_shift : row_shift + span_rows, col_shift : col_shift + span_cols]
            kept_mask = near_mask[:, :, row_shift * 3 + col_shift].astype(points.dtype)
            windows.append(source * kept_mask[:, :, None, None])
    stacked = jnp.concatenate(windows, 3)
    joined_table = matrices.reshape(9 * 2 * LEAF, 2 * LEAF)
    near = jnp.einsum("ijsp,pq->ijsq", stacked, joined_table, preferred_element_type=jnp.float32)
    return near.reshape(span_rows, span_cols, SIDES, LEAF)


def apply_operator(
    field,
    leaf_basis,
    transfer,
    coupling,
    near_table,
    near_mask,
    mask_leaf,
    mask_mid,
    mask_upper,
    mask_top,
):
    span_rows, span_cols = (field.shape[0], field.shape[1])
    points = field.reshape(span_rows, span_cols, SIDES, LEAF)
    basis_mat = leaf_basis.reshape(span_rows, span_cols, LEAF, RANK)
    leaf_coeffs = jnp.einsum(
        "ijsp,ijpr->ijsr", points, basis_mat, preferred_element_type=jnp.float32
    )
    leaf_coeffs = leaf_coeffs.astype(jnp.bfloat16).reshape(span_rows, span_cols, SIDES * RANK)
    field_pad = with_halo(field, (("br", 1), (("rhs", "sub"), 0)), 1)
    leaf_pad = with_halo(leaf_coeffs, (("br", 1), (("rhs", "sub"), 0)), 2)
    mid_coeffs = upward(leaf_coeffs, transfer[0])
    mid_pad = with_halo(mid_coeffs, (("br", 1), (("rhs", "sub"), 0)), 2)
    upper_coeffs = upward(mid_coeffs, transfer[1])
    row_index = lax.axis_index(("rhs", "sub"))
    upper_rows = upper_coeffs.shape[0]
    top_rows = upper_rows // 2
    upper_pad = with_halo(upper_coeffs, (("br", 1), (("rhs", "sub"), 0)), 2)
    upper_mask = lax.dynamic_slice_in_dim(mask_upper, row_index * upper_rows, upper_rows, 0)
    upper_local = couple_block(upper_pad, upper_mask, coupling[2])
    top_coeffs = upward(upper_coeffs, transfer[2])
    top_column = lax.all_gather(top_coeffs, ("rhs", "sub"), axis=0, tiled=True)
    top_wide = with_halo(top_column, (("br", 1),), 2)
    top_local = column_couple(top_wide, mask_top, coupling[3], row_index * top_rows, top_rows)
    upper_local = upper_local + downward(top_local, transfer[2])
    mid_local = couple_block(mid_pad, mask_mid, coupling[1]) + downward(upper_local, transfer[1])
    leaf_local = couple_block(leaf_pad, mask_leaf, coupling[0]) + downward(mid_local, transfer[0])
    near = near_field(field_pad, near_table, near_mask)
    leaf_half = leaf_local.astype(jnp.bfloat16).reshape(span_rows, span_cols, SIDES, RANK)
    far_part = jnp.einsum(
        "ijsr,ijpr->ijsp", leaf_half, basis_mat, preferred_element_type=jnp.float32
    )
    return (near + far_part).reshape(span_rows, span_cols, SIDES * LEAF).astype(jnp.bfloat16)


def on_device(
    sources,
    leaf_basis,
    transfer,
    coupling,
    near_table,
    near_mask,
    mask_leaf,
    mask_mid,
    mask_upper,
    mask_top,
):
    field = sources
    for product_step in range(PRODUCTS):
        field = apply_operator(
            field,
            leaf_basis,
            transfer,
            coupling,
            near_table,
            near_mask,
            mask_leaf,
            mask_mid,
            mask_upper,
            mask_top,
        )
    return field


def solution(mesh):
    placed = (
        P(("grp", "rhs", "sub"), "br", None),
        P(("grp", "rhs", "sub"), "br", None),
        P(),
        P(),
        P(),
        P(("grp", "rhs", "sub"), "br", None),
        P(("grp", "rhs", "sub"), "br", None),
        P(("grp", "rhs", "sub"), "br", None),
        P("grp", "br", None),
        P("grp", "br", None),
    )
    return jax.shard_map(
        on_device,
        mesh=mesh,
        in_specs=placed,
        out_specs=P(("grp", "rhs", "sub"), "br", None),
        check_vma=False,
    )
```

profile of v0, /device:TPU:15, one launch (start us, length us, event | category | flops | bytes accessed | tf_op | source)
XLA Modules:
  0.0 2027.7 jit_solution(9908582315812842184)
XLA Ops:
  0.0 3.3 reshape.4098
  16.8 6.1 all_gather.9
  41.9 11.3 slice_reduce_fusion.3
  63.2 13.3 broadcast_multiply_fusion.3
  1177.4 3.4 collective-permute-start.13
  1276.8 7.8 collective-permute-start.15
  1288.0 4.9 collective-permute-start.11
  1295.9 4.3 collective-permute-start.3
  1382.2 4.7 collective-permute-start.7
  1462.6 6.5 all_gather.10
  1492.5 3.4 collective-permute-start.26
  1502.2 3.4 collective-permute-start.18
  1586.6 6.6 collective-permute-start.33
  1595.7 4.9 collective-permute-start.29
  1603.5 3.7 collective-permute-start.21
  1668.8 5.3 collective-permute-start.25
  1748.3 6.5 all_gather.11
  1778.2 3.4 collective-permute-start.44
  1787.9 3.4 collective-permute-start.36
  1872.3 6.6 collective-permute-start.51
  1881.4 4.9 collective-permute-start.47
  1889.3 3.7 collective-permute-start.39
  1954.5 5.3 collective-permute-start.43
  2020.8 3.8 add_convert_fusion
  (3731 shorter events, 1881.4 us)
Async XLA Ops:
  22.9 1173.8 %collective-permute-start.16 = (bf16[4,2,2048]{2,1,0:T(2,128)(2,1)}, bf16[4,2,2048]{2,1,0:T(2,128)(2,1)}, u32[]{:S(2)}, u32[]{:S(2)}) collective-permute-start(bf16[4,2,2048]{2,1,0:T(2,128)(2,1)} %all_gather.9), channel_id=1, source_target_pairs={{0,4},{4,8},{8,12},{1,5},{5,9},{9,13},{2,6},{6,10},{10,14},{3,7},{... | collective-permute-start | bytes 98312 | tf_op jit(solution)/shard_map/ppermute | solution.py:17
  26.1 1173.1 %collective-permute-start.17 = (bf16[4,2,2048]{2,1,0:T(2,128)(2,1)}, bf16[4,2,2048]{2,1,0:T(2,128)(2,1)}, u32[]{:S(2)}, u32[]{:S(2)}) collective-permute-start(bf16[4,2,2048]{2,1,0:T(2,128)(2,1)} %all_gather.9), channel_id=1, source_target_pairs={{4,0},{8,4},{12,8},{5,1},{9,5},{13,9},{6,2},{10,6},{14,10},{7,3},{... | collective-permute-start | bytes 98312 | tf_op jit(solution)/shard_map/ppermute | solution.py:20
  32.2 1255.9 %collective-permute-start.4 = (bf16[8,2,2048]{2,1,0:T(2,128)(2,1)}, bf16[8,2,2048]{2,1,0:T(2,128)(2,1)}, u32[]{:S(2)}, u32[]{:S(2)}) collective-permute-start(bf16[8,2,2048]{2,1,0:T(2,128)(2,1)} %get-tuple-element.216), channel_id=1, source_target_pairs={{0,4},{4,8},{8,12},{1,5},{5,9},{9,13},{2,6},{6,10},{10,14},{3,7},{... | collective-permute-start | bytes 196616 | tf_op jit(solution)/shard_map/ppermute | solution.py:17
  34.8 1258.1 %collective-permute-start.5 = (bf16[8,2,2048]{2,1,0:T(2,128)(2,1)}, bf16[8,2,2048]{2,1,0:T(2,128)(2,1)}, u32[]{:S(2)}, u32[]{:S(2)}) collective-permute-start(bf16[8,2,2048]{2,1,0:T(2,128)(2,1)} %get-tuple-element.217), channel_id=1, source_target_pairs={{4,0},{8,4},{12,8},{5,1},{9,5},{13,9},{6,2},{10,6},{14,10},{7,3},{... | collective-permute-start | bytes 196616 | tf_op jit(solution)/shard_map/ppermute | solution.py:20
  39.5 1138.0 %collective-permute-start.12 = (bf16[2,2,2048]{2,0,1:T(2,128)(2,1)}, bf16[2,2,2048]{2,0,1:T(2,128)(2,1)}, u32[]{:S(2)}, u32[]{:S(2)}) collective-permute-start(bf16[2,2,2048]{2,0,1:T(2,128)(2,1)} %get-tuple-element.1130), channel_id=1, source_target_pairs={{0,4},{4,8},{8,12},{1,5},{5,9},{9,13},{2,6},{6,10},{10,14},{3,7},{... | collective-permute-start | bytes 49160 | tf_op jit(solution)/shard_map/ppermute | solution.py:17
  1196.7 87.9 %collective-permute-start.1 = (bf16[8,1,2048]{2,1,0:T(2,128)(2,1)}, bf16[8,1,2048]{2,1,0:T(2,128)(2,1)}, u32[]{:S(2)}, u32[]{:S(2)}) collective-permute-start(bf16[8,1,2048]{2,1,0:T(2,128)(2,1)} %get-tuple-element.219), channel_id=1, source_target_pairs={{4,0},{8,4},{12,8},{5,1},{9,5},{13,9},{6,2},{10,6},{14,10},{7,3},{... | collective-permute-start | bytes 98312 | tf_op jit(solution)/shard_map/ppermute | solution.py:20
  1199.2 96.7 %collective-permute-start.14 = (bf16[2,8,2048]{2,0,1:T(2,128)(2,1)}, bf16[2,8,2048]{2,0,1:T(2,128)(2,1)}, u32[]{:S(2)}, u32[]{:S(2)}) collective-permute-start(bf16[2,8,2048]{2,0,1:T(2,128)(2,1)} %constant_dynamic-update-slice_fusion.444), channel_id=1, source_target_pairs={{0,1},{1,2},{2,3},{4,5},{5,6},{6,7},{8,9},{9,10},{10,11},{12,13},{... | collective-permute-start | bytes 196616 | tf_op jit(solution)/shard_map/ppermute | solution.py:17
  1284.6 113.5 %collective-permute-start.10 = (bf16[2,12,2048]{2,0,1:T(2,128)(2,1)}, bf16[2,12,2048]{2,0,1:T(2,128)(2,1)}, u32[]{:S(2)}, u32[]{:S(2)}) collective-permute-start(bf16[2,12,2048]{2,0,1:T(2,128)(2,1)} %get-tuple-element.338), channel_id=1, source_target_pairs={{0,1},{1,2},{2,3},{4,5},{5,6},{6,7},{8,9},{9,10},{10,11},{12,13},{... | collective-permute-start | bytes 294920 | tf_op jit(solution)/shard_map/ppermute | solution.py:17
  1288.0 110.1 %collective-permute-start.11 = (bf16[2,12,2048]{2,0,1:T(2,128)(2,1)}, bf16[2,12,2048]{2,0,1:T(2,128)(2,1)}, u32[]{:S(2)}, u32[]{:S(2)}) collective-permute-start(bf16[2,12,2048]{2,0,1:T(2,128)(2,1)} %get-tuple-element.339), channel_id=1, source_target_pairs={{1,0},{2,1},{3,2},{5,4},{6,5},{7,6},{9,8},{10,9},{11,10},{13,12},{... | collective-permute-start | bytes 294920 | tf_op jit(solution)/shard_map/ppermute | solution.py:20
  1292.9 89.2 %collective-permute-start.2 = (bf16[1,18,2048]{2,1,0:T(8,128)(2,1)}, bf16[1,18,2048]{2,1,0:T(8,128)(2,1)}, u32[]{:S(2)}, u32[]{:S(2)}) collective-permute-start(bf16[1,18,2048]{2,1,0:T(8,128)(2,1)} %get-tuple-element.206), channel_id=1, source_target_pairs={{0,1},{1,2},{2,3},{4,5},{5,6},{6,7},{8,9},{9,10},{10,11},{12,13},{... | collective-permute-start | bytes 221192 | tf_op jit(solution)/shard_map/ppermute | solution.py:17
  1295.9 90.9 %collective-permute-start.3 = (bf16[1,18,2048]{2,1,0:T(8,128)(2,1)}, bf16[1,18,2048]{2,1,0:T(8,128)(2,1)}, u32[]{:S(2)}, u32[]{:S(2)}) collective-permute-start(bf16[1,18,2048]{2,1,0:T(8,128)(2,1)} %get-tuple-element.207), channel_id=1, source_target_pairs={{1,0},{2,1},{3,2},{5,4},{6,5},{7,6},{9,8},{10,9},{11,10},{13,12},{... | collective-permute-start | bytes 221192 | tf_op jit(solution)/shard_map/ppermute | solution.py:20
  1300.2 119.0 %collective-permute-start.6 = (bf16[2,20,2048]{2,1,0:T(8,128)(2,1)}, bf16[2,20,2048]{2,1,0:T(8,128)(2,1)}, u32[]{:S(2)}, u32[]{:S(2)}) collective-permute-start(bf16[2,20,2048]{2,1,0:T(8,128)(2,1)} %get-tuple-element.204), channel_id=1, source_target_pairs={{0,1},{1,2},{2,3},{4,5},{5,6},{6,7},{8,9},{9,10},{10,11},{12,13},{... | collective-permute-start | bytes 491528 | tf_op jit(solution)/shard_map/ppermute | solution.py:17
  1480.1 115.5 %collective-permute-start.22 = (bf16[8,2,2048]{2,1,0:T(2,128)(2,1)}, bf16[8,2,2048]{2,1,0:T(2,128)(2,1)}, u32[]{:S(2)}, u32[]{:S(2)}) collective-permute-start(bf16[8,2,2048]{2,1,0:T(2,128)(2,1)} %get-tuple-element.212), channel_id=1, source_target_pairs={{0,4},{4,8},{8,12},{1,5},{5,9},{9,13},{2,6},{6,10},{10,14},{3,7},{... | collective-permute-start | bytes 196616 | tf_op jit(solution)/shard_map/ppermute | solution.py:17
  1490.6 110.0 %collective-permute-start.23 = (bf16[8,2,2048]{2,1,0:T(2,128)(2,1)}, bf16[8,2,2048]{2,1,0:T(2,128)(2,1)}, u32[]{:S(2)}, u32[]{:S(2)}) collective-permute-start(bf16[8,2,2048]{2,1,0:T(2,128)(2,1)} %get-tuple-element.213), channel_id=1, source_target_pairs={{4,0},{8,4},{12,8},{5,1},{9,5},{13,9},{6,2},{10,6},{14,10},{7,3},{... | collective-permute-start | bytes 196616 | tf_op jit(solution)/shard_map/ppermute | solution.py:20
  1509.0 94.6 %collective-permute-start.32 = (bf16[2,8,2048]{2,1,0:T(8,128)(2,1)}, bf16[2,8,2048]{2,1,0:T(8,128)(2,1)}, u32[]{:S(2)}, u32[]{:S(2)}) collective-permute-start(bf16[2,8,2048]{2,1,0:T(8,128)(2,1)} %pad_maximum_fusion.25), channel_id=1, source_target_pairs={{0,1},{1,2},{2,3},{4,5},{5,6},{6,7},{8,9},{9,10},{10,11},{12,13},{... | collective-permute-start | bytes 196616 | tf_op jit(solution)/shard_map/ppermute | solution.py:17
  1593.2 90.7 %collective-permute-start.28 = (bf16[2,12,2048]{2,0,1:T(2,128)(2,1)}, bf16[2,12,2048]{2,0,1:T(2,128)(2,1)}, u32[]{:S(2)}, u32[]{:S(2)}) collective-permute-start(bf16[2,12,2048]{2,0,1:T(2,128)(2,1)} %get-tuple-element.327), channel_id=1, source_target_pairs={{0,1},{1,2},{2,3},{4,5},{5,6},{6,7},{8,9},{9,10},{10,11},{12,13},{... | collective-permute-start | bytes 294920 | tf_op jit(solution)/shard_map/ppermute | solution.py:17
  1595.7 88.2 %collective-permute-start.29 = (bf16[2,12,2048]{2,0,1:T(2,128)(2,1)}, bf16[2,12,2048]{2,0,1:T(2,128)(2,1)}, u32[]{:S(2)}, u32[]{:S(2)}) collective-permute-start(bf16[2,12,2048]{2,0,1:T(2,128)(2,1)} %get-tuple-element.328), channel_id=1, source_target_pairs={{1,0},{2,1},{3,2},{5,4},{6,5},{7,6},{9,8},{10,9},{11,10},{13,12},{... | collective-permute-start | bytes 294920 | tf_op jit(solution)/shard_map/ppermute | solution.py:20
  1607.2 97.7 %collective-permute-start.24 = (bf16[2,20,2048]{2,1,0:T(8,128)(2,1)}, bf16[2,20,2048]{2,1,0:T(8,128)(2,1)}, u32[]{:S(2)}, u32[]{:S(2)}) collective-permute-start(bf16[2,20,2048]{2,1,0:T(8,128)(2,1)} %get-tuple-element.200), channel_id=1, source_target_pairs={{0,1},{1,2},{2,3},{4,5},{5,6},{6,7},{8,9},{9,10},{10,11},{12,13},{... | collective-permute-start | bytes 491528 | tf_op jit(solution)/shard_map/ppermute | solution.py:17
  1765.9 115.5 %collective-permute-start.40 = (bf16[8,2,2048]{2,1,0:T(2,128)(2,1)}, bf16[8,2,2048]{2,1,0:T(2,128)(2,1)}, u32[]{:S(2)}, u32[]{:S(2)}) collective-permute-start(bf16[8,2,2048]{2,1,0:T(2,128)(2,1)} %get-tuple-element.208), channel_id=1, source_target_pairs={{0,4},{4,8},{8,12},{1,5},{5,9},{9,13},{2,6},{6,10},{10,14},{3,7},{... | collective-permute-start | bytes 196616 | tf_op jit(solution)/shard_map/ppermute | solution.py:17
  1776.3 110.0 %collective-permute-start.41 = (bf16[8,2,2048]{2,1,0:T(2,128)(2,1)}, bf16[8,2,2048]{2,1,0:T(2,128)(2,1)}, u32[]{:S(2)}, u32[]{:S(2)}) collective-permute-start(bf16[8,2,2048]{2,1,0:T(2,128)(2,1)} %get-tuple-element.209), channel_id=1, source_target_pairs={{4,0},{8,4},{12,8},{5,1},{9,5},{13,9},{6,2},{10,6},{14,10},{7,3},{... | collective-permute-start | bytes 196616 | tf_op jit(solution)/shard_map/ppermute | solution.py:20
  1794.7 94.6 %collective-permute-start.50 = (bf16[2,8,2048]{2,1,0:T(8,128)(2,1)}, bf16[2,8,2048]{2,1,0:T(8,128)(2,1)}, u32[]{:S(2)}, u32[]{:S(2)}) collective-permute-start(bf16[2,8,2048]{2,1,0:T(8,128)(2,1)} %pad_maximum_fusion.26), channel_id=1, source_target_pairs={{0,1},{1,2},{2,3},{4,5},{5,6},{6,7},{8,9},{9,10},{10,11},{12,13},{... | collective-permute-start | bytes 196616 | tf_op jit(solution)/shard_map/ppermute | solution.py:17
  1878.9 90.7 %collective-permute-start.46 = (bf16[2,12,2048]{2,0,1:T(2,128)(2,1)}, bf16[2,12,2048]{2,0,1:T(2,128)(2,1)}, u32[]{:S(2)}, u32[]{:S(2)}) collective-permute-start(bf16[2,12,2048]{2,0,1:T(2,128)(2,1)} %get-tuple-element.316), channel_id=1, source_target_pairs={{0,1},{1,2},{2,3},{4,5},{5,6},{6,7},{8,9},{9,10},{10,11},{12,13},{... | collective-permute-start | bytes 294920 | tf_op jit(solution)/shard_map/ppermute | solution.py:17
  1881.4 88.2 %collective-permute-start.47 = (bf16[2,12,2048]{2,0,1:T(2,128)(2,1)}, bf16[2,12,2048]{2,0,1:T(2,128)(2,1)}, u32[]{:S(2)}, u32[]{:S(2)}) collective-permute-start(bf16[2,12,2048]{2,0,1:T(2,128)(2,1)} %get-tuple-element.317), channel_id=1, source_target_pairs={{1,0},{2,1},{3,2},{5,4},{6,5},{7,6},{9,8},{10,9},{11,10},{13,12},{... | collective-permute-start | bytes 294920 | tf_op jit(solution)/shard_map/ppermute | solution.py:20
  1892.9 97.1 %collective-permute-start.42 = (bf16[2,20,2048]{2,1,0:T(8,128)(2,1)}, bf16[2,20,2048]{2,1,0:T(8,128)(2,1)}, u32[]{:S(2)}, u32[]{:S(2)}) collective-permute-start(bf16[2,20,2048]{2,1,0:T(8,128)(2,1)} %get-tuple-element.196), channel_id=1, source_target_pairs={{0,1},{1,2},{2,3},{4,5},{5,6},{6,7},{8,9},{9,10},{10,11},{12,13},{... | collective-permute-start | bytes 491528 | tf_op jit(solution)/shard_map/ppermute | solution.py:17
  (725 other events, 17859.0 us)
where the time goes:
time: 2060 us; the launch traced here: 2030 us
  other arithmetic  978 us (47%)
  local copies, waits for them, and re-layouts  771 us (37%)
  starting transfers between devices  160 us (8%)
  matrix products  72.4 us (4%)
    unnamed x1006, other arithmetic  477 us
    slice x324, other arithmetic, couple_block(): slot_mask[row_par::2, col_par::2, slot_index].astype(coeffs.dtype)  426 us
    slice x330, local copies, waits for them, and re-layouts, couple_block(): slot_mask[row_par::2, col_par::2, slot_index].astype(coeffs.dtype)  308 us
    squeeze x160, local copies, waits for them, and re-layouts, couple_block(): tables.append(matrices[(row_step + 3) * 7 + col_step + 3])  236 us
    ppermute x27, starting transfers between devices, with_halo(): lax.ppermute(lax.slice_in_dim(block, 0, width, axis=dim), axis, backward)  99.5 us
    unnamed x1555, local copies, waits for them, and re-layouts  94.1 us
    ppermute x27, starting transfers between devices, with_halo(): lax.ppermute(lax.slice_in_dim(block, block.shape[dim] - width, None, axis...  60.4 us
    dot_general x48, matrix products, couple_block(): jnp.einsum('ijsr,rt->ijst', stacked, joined_table, preferred_element_type...  47.9 us
  transfers between devices with their start and end apart: 54, of which 6 were waited for; matrix products, arithmetic and copies ran while one was open for 83% of the time, Pallas kernels for 0%

commit v1 on v0

v1 whole, which is shorter than its diff:
```python
import functools

import jax
import jax.numpy as jnp
from jax import lax
from jax.experimental import pallas as pl
from jax.experimental.pallas import tpu as pltpu
from jax.sharding import PartitionSpec as P

LEAF = 64
RANK = 64
SIDES = 32
PRODUCTS = 3
PAIRS = SIDES // 2
WIDE = 2 * RANK
SLOTS = 27
ROW_AXES = ("rhs", "sub")
BF16 = jnp.bfloat16
F32 = jnp.float32


def window_slots(row_par, col_par):
    slots = []
    for a in range(6):
        for b in range(6):
            if abs(a - 2 - row_par) <= 1 and abs(b - 2 - col_par) <= 1:
                continue
            slots.append((a, b))
    return slots


def offset_index(slot, row_par, col_par):
    return 7 * (slot[0] + 1 - row_par) + slot[1] + 1 - col_par


CLASSES = [(row_par, col_par) for row_par in range(2) for col_par in range(2)]


def paired(matrices):
    zeros = jnp.zeros_like(matrices)
    upper = jnp.concatenate([matrices, zeros], -1)
    lower = jnp.concatenate([zeros, matrices], -1)
    return jnp.concatenate([upper, lower], -2)


def window_index(slot_mask, rows, cols):
    width = cols + 4
    zero_tile = (rows + 4) * width
    parts = []
    for row_par, col_par in CLASSES:
        slots = window_slots(row_par, col_par)
        first = jnp.asarray([a * width + b for a, b in slots], jnp.int32)
        row = jnp.arange(rows // 2, dtype=jnp.int32)[:, None, None] * (2 * width)
        col = jnp.arange(cols // 2, dtype=jnp.int32)[None, :, None] * 2
        kept = slot_mask[row_par::2, col_par::2] != 0
        parts.append(jnp.where(kept, row + col + first, zero_tile).reshape(-1))
    return parts


def near_index(near_mask, rows, cols):
    width = cols + 2
    first = jnp.asarray([u * width + v for u in range(3) for v in range(3)], jnp.int32)
    row = jnp.arange(rows, dtype=jnp.int32)[:, None, None] * width
    col = jnp.arange(cols, dtype=jnp.int32)[None, :, None]
    index = jnp.where(near_mask != 0, row + col + first, (rows + 2) * width)
    return [index[row_par::2, col_par::2].reshape(-1) for row_par, col_par in CLASSES]


def top_index(mask_top, row, count):
    parity = row % 2
    mask_row = lax.dynamic_slice_in_dim(mask_top, row, 1, 0)[0]
    place = [2, 3, 0, 1, 4, 5]
    tiles, tables = [], []
    for col_par in range(2):
        lists = [window_slots(row_par, col_par) for row_par in range(2)]
        a, b, o = [
            jnp.where(parity == 0, jnp.asarray(even, jnp.int32), jnp.asarray(odd, jnp.int32))
            for even, odd in (
                ([s[0] for s in lists[0]], [s[0] for s in lists[1]]),
                ([place[s[1]] for s in lists[0]], [place[s[1]] for s in lists[1]]),
                (
                    [offset_index(s, 0, col_par) for s in lists[0]],
                    [offset_index(s, 1, col_par) for s in lists[1]],
                ),
            )
        ]
        source = row - parity + a - 2
        kept = (mask_row[col_par] != 0) & (source >= 0) & (source < count)
        tiles.append(jnp.where(kept, source * 6 + b, 6 * count))
        tables.append(o)
    return tiles + tables


def dot(a, b):
    return jnp.dot(a, b, preferred_element_type=F32)


def dot_t(a, b):
    return lax.dot_general(a, b, (((1,), (1,)), ((), ())), preferred_element_type=F32)


def halves(ref):
    rows, cols = ref.shape[0], ref.shape[1]
    return ref.reshape(rows // 2, 2, cols // 2, 2, PAIRS, WIDE)


def tiles_of(value):
    return value.reshape(-1, WIDE)


def climb(child, parent, table, level):
    rows, cols = parent.shape[0], parent.shape[1]
    total = None
    for c, (a, b) in enumerate(CLASSES):
        block = tiles_of(halves(child)[:, a, :, b])
        part = dot(block, table[level, c])
        total = part if total is None else total + part
    parent[...] = total.astype(BF16).reshape(rows, cols, PAIRS, WIDE)


def upward_pass(field, basis, up_table, q0, q1, q2, q3, send_l, send_r, send_u, send_d):
    rows, cols = field.shape[0], field.shape[1]

    def leaf_row(i, carry):
        for j in range(cols):
            q0[i, j] = dot(field[i, j], basis[i * cols + j]).astype(BF16)
        return carry

    lax.fori_loop(0, rows, leaf_row, 0)
    climb(q0, q1, up_table, 0)
    climb(q1, q2, up_table, 1)
    climb(q2, q3, up_table, 2)
    for ref, side in ((send_l, 0), (send_r, 1)):
        at = 0
        for source, first, last, width in col_message(rows):
            level = (q0, q1, q2, q3, field)[source]
            low = 0 if side == 0 else level.shape[1] - width
            for r in range(first, last):
                ref[at : at + width] = level[r, low : low + width]
                at += width
    for ref, side in ((send_u, 0), (send_d, 1)):
        at = 0
        for level, width in ((q0, 2), (field, 1), (q1, 2), (q2, 2)):
            low = 0 if side == 0 else level.shape[0] - width
            for r in range(low, low + width):
                ref[at : at + level.shape[1]] = level[r]
                at += level.shape[1]


def col_message(rows):
    return [
        (0, 2, rows - 2, 2),
        (4, 1, rows - 1, 1),
        (0, 0, 2, 2),
        (4, 0, 1, 1),
        (1, 0, 2, 2),
        (2, 0, rows // 4, 2),
        (0, rows - 2, rows, 2),
        (4, rows - 1, rows, 1),
        (1, rows // 2 - 2, rows // 2, 2),
        (3, 0, rows // 8, 2),
    ]


def message_sizes(rows):
    counts = [(last - first) * width for _, first, last, width in col_message(rows)]
    start = sum(counts[:2])
    up = (start, start + sum(counts[2:6]))
    down = (start + sum(counts[2:5]), start + sum(counts[2:9]))
    return counts, up, down


def fill_windows(own, recv_l, recv_r, recv_u, recv_d, pads):
    q0, q1, q2, field = own
    p0, p1, p2, pf = pads
    rows = q0.shape[0]
    zero = jnp.zeros((PAIRS, WIDE), BF16)

    def place(level):
        ref, halo = {0: (p0, 2), 1: (p1, 2), 2: (p2, 2), 4: (pf, 1)}[level]
        source = {0: q0, 1: q1, 2: q2, 4: field}[level]
        return ref, halo, source.shape[0], source.shape[1]

    for level, source in ((0, q0), (1, q1), (2, q2), (4, field)):
        ref, halo, level_rows, level_cols = place(level)
        width = level_cols + 2 * halo
        ref[(level_rows + 2 * halo) * width] = zero
        for r in range(level_rows):
            start = (r + halo) * width + halo
            ref[start : start + level_cols] = source[r]
    for recv, side in ((recv_l, 0), (recv_r, 1)):
        at = 0
        for level, first, last, count in col_message(rows)[:-1]:
            ref, halo, level_rows, level_cols = place(level)
            width = level_cols + 2 * halo
            for r in range(first, last):
                start = (r + halo) * width + (0 if side == 0 else halo + level_cols)
                ref[start : start + count] = recv[at : at + count]
                at += count
    for recv, side in ((recv_u, 0), (recv_d, 1)):
        at = 0
        for level in (0, 4, 1, 2):
            ref, halo, level_rows, level_cols = place(level)
            width = level_cols + 2 * halo
            for r in range(halo):
                row = r if side == 0 else halo + level_rows + r
                start = row * width + halo
                ref[start : start + level_cols] = recv[at : at + level_cols]
                at += level_cols
        corner = (2, 0, 4, 1) if side == 0 else (0, 4, 1, 2)
        for edge in range(2):
            for level in corner:
                ref, halo, level_rows, level_cols = place(level)
                width = level_cols + 2 * halo
                for r in range(halo):
                    row = r if side == 0 else halo + level_rows + r
                    start = row * width + (0 if edge == 0 else halo + level_cols)
                    ref[start : start + halo] = recv[at : at + halo]
                    at += halo


def gather(index, base, count, slots, source, lhs):
    def one(n, carry):
        at = base + n * slots
        for k in range(slots):
            lhs[n, :, k * WIDE : (k + 1) * WIDE] = source[index[at + k]]
        return carry

    lax.fori_loop(0, count, one, 0)


def contract(lhs, count, tables, chunk=4):
    total = None
    for start in range(0, len(tables), chunk):
        group = tables[start : start + chunk]
        block = lhs[0:count, :, start * WIDE : (start + len(group)) * WIDE]
        weights = jnp.concatenate([read() for read in group], 0)
        part = dot(block.reshape(count * PAIRS, len(group) * WIDE), weights)
        total = part if total is None else total + part
    return total


def far_level(level, index, base, source, table, down_table, parent, lhs, out):
    rows, cols = out.shape[0], out.shape[1]
    count = rows * cols // 4
    for c, (row_par, col_par) in enumerate(CLASSES):
        slots = window_slots(row_par, col_par)
        gather(index, base + c * count * SLOTS, count, SLOTS, source, lhs)
        lhs[0:count, :, SLOTS * WIDE : (SLOTS + 1) * WIDE] = parent[...].reshape(
            count, PAIRS, WIDE
        )
        reads = [
            functools.partial(lambda o: table[o], offset_index(s, row_par, col_par)) for s in slots
        ]
        reads.append(functools.partial(lambda k: down_table[level, k], c))
        total = contract(lhs, count, reads)
        halves(out)[:, row_par, :, col_par] = total.astype(BF16).reshape(
            rows // 2, cols // 2, PAIRS, WIDE
        )


def product_kernel(last, sizes, *refs):
    (
        index, field, q0, q1, q2, column, recv_l, recv_r, recv_u, recv_d,
        tab0, tab1, tab2, tab3, up_table, down_table, near_table, basis,
    ) = refs[:18]
    outs = refs[18 : 19 if last else 27]
    p0, p1, p2, p3, pf, g0, g1, g2, g3, near, lhs = refs[19 if last else 27 :]
    rows, cols = field.shape[0], field.shape[1]
    count = column.shape[0]
    fill_windows((q0, q1, q2, field), recv_l, recv_r, recv_u, recv_d, (p0, p1, p2, pf))
    p3[0:count] = column[...]
    p3[count] = jnp.zeros((PAIRS, WIDE), BF16)
    base_near, base0, base1, base2, base3, base_top = sizes
    for j in range(2):
        for k in range(SLOTS):
            lhs[0, :, k * WIDE : (k + 1) * WIDE] = p3[index[base3 + j * SLOTS + k]]
        reads = [
            functools.partial(lambda k: tab3[index[k]], base_top + j * SLOTS + k)
            for k in range(SLOTS)
        ]
        g3[0, j] = contract(lhs, 1, reads).astype(BF16)
    far_level(2, index, base2, p2, tab2, down_table, g3, lhs, g2)
    far_level(1, index, base1, p1, tab1, down_table, g2, lhs, g1)
    far_level(0, index, base0, p0, tab0, down_table, g1, lhs, g0)
    quarter = rows * cols // 4
    for c, (row_par, col_par) in enumerate(CLASSES):
        gather(index, base_near + c * quarter * 9, quarter, 9, pf, lhs)
        reads = [functools.partial(lambda k: near_table[k], k) for k in range(9)]
        total = contract(lhs, quarter, reads)
        halves(near)[:, row_par, :, col_par] = total.reshape(rows // 2, cols // 2, PAIRS, WIDE)
    result = outs[0]

    def leaf_row(i, carry):
        for j in range(cols):
            far = dot_t(g0[i, j], basis[i * cols + j])
            result[i, j] = (near[i, j] + far).astype(BF16)
        return carry

    lax.fori_loop(0, rows, leaf_row, 0)
    if not last:
        upward_pass(result, basis, up_table, *outs[1:])


def first_kernel(field, basis, up_table, *outs):
    upward_pass(field, basis, up_table, *outs)


def shape_of(*dims):
    return jax.ShapeDtypeStruct(tuple(dims) + (PAIRS, WIDE), BF16)


def upward_shapes(rows, cols):
    counts, _, _ = message_sizes(rows)
    edge = 2 * cols + cols + cols + cols // 2
    return [
        shape_of(rows, cols),
        shape_of(rows // 2, cols // 2),
        shape_of(rows // 4, cols // 4),
        shape_of(rows // 8, cols // 8),
        shape_of(sum(counts)),
        shape_of(sum(counts)),
        shape_of(edge),
        shape_of(edge),
    ]


VMEM = pl.BlockSpec(memory_space=pltpu.VMEM)
SMEM = pl.BlockSpec(memory_space=pltpu.SMEM)
PARAMS = pltpu.CompilerParams(vmem_limit_bytes=48 * 1024 * 1024)


def start_up(field, basis, up_table):
    outs = upward_shapes(field.shape[0], field.shape[1])
    return pl.pallas_call(
        first_kernel,
        out_shape=outs,
        in_specs=[VMEM] * 3,
        out_specs=[VMEM] * len(outs),
        compiler_params=PARAMS,
    )(field, basis, up_table)


def product(last, sizes, index, field, q0, q1, q2, column, received, tables):
    rows, cols = field.shape[0], field.shape[1]
    outs = [shape_of(rows, cols)]
    if not last:
        outs += upward_shapes(rows, cols)

    def tile_scratch(*dims):
        return pltpu.VMEM(tuple(dims) + (PAIRS, WIDE), BF16)

    args = (index, field, q0, q1, q2, column, *received, *tables)
    result = pl.pallas_call(
        functools.partial(product_kernel, last, sizes),
        out_shape=outs,
        in_specs=[SMEM] + [VMEM] * (len(args) - 1),
        out_specs=[VMEM] * len(outs),
        scratch_shapes=[
            tile_scratch((rows + 4) * (cols + 4) + 1),
            tile_scratch((rows // 2 + 4) * (cols // 2 + 4) + 1),
            tile_scratch((rows // 4 + 4) * (cols // 4 + 4) + 1),
            tile_scratch(column.shape[0] + 1),
            tile_scratch((rows + 2) * (cols + 2) + 1),
            tile_scratch(rows, cols),
            tile_scratch(rows // 2, cols // 2),
            tile_scratch(rows // 4, cols // 4),
            tile_scratch(rows // 8, cols // 8),
            pltpu.VMEM((rows, cols, PAIRS, WIDE), F32),
            pltpu.VMEM((rows * cols // 4, PAIRS, (SLOTS + 1) * WIDE), BF16),
        ],
        compiler_params=PARAMS,
    )(*args)
    return result


def shift(value, axis, step):
    count = lax.axis_size(axis)
    pairs = [(i, i + step) for i in range(count) if 0 <= i + step < count]
    return lax.ppermute(value, axis, pairs)


def exchange(rows, q3, send_l, send_r, send_u, send_d):
    counts, up, down = message_sizes(rows)
    recv_l = shift(send_r, "br", 1)
    recv_r = shift(send_l, "br", -1)
    up_message = jnp.concatenate([send_u, recv_l[up[0] : up[1]], recv_r[up[0] : up[1]]], 0)
    down_message = jnp.concatenate(
        [send_d, recv_l[down[0] : down[1]], recv_r[down[0] : down[1]]], 0
    )
    recv_d = shift(up_message, ROW_AXES, -1)
    recv_u = shift(down_message, ROW_AXES, 1)
    last = down[1]
    wide = jnp.concatenate([q3[0], recv_l[last:], recv_r[last:]], 0)
    column = lax.all_gather(wide, ROW_AXES, axis=0, tiled=True)
    return column, (recv_l, recv_r, recv_u, recv_d)


def on_device(
    sources, leaf_basis, transfer, coupling, near_table, near_mask,
    mask_leaf, mask_mid, mask_upper, mask_top,
):
    rows, cols = sources.shape[0], sources.shape[1]
    row = lax.axis_index(ROW_AXES)
    row_count = lax.axis_size(ROW_AXES)
    field = sources.reshape(rows, cols, PAIRS, WIDE)
    basis = paired(leaf_basis.reshape(rows * cols, LEAF, RANK))
    tables = paired(coupling.reshape(4, 49, RANK, RANK))
    moves = transfer.reshape(3, 4, RANK, RANK)
    up_table = paired(moves)
    down_table = paired(jnp.swapaxes(moves, 2, 3))
    near_pair = paired(near_table.reshape(9, LEAF, LEAF))
    upper = lax.dynamic_slice_in_dim(mask_upper, row * (rows // 4), rows // 4, 0)
    lists = [
        near_index(near_mask, rows, cols),
        window_index(mask_leaf, rows, cols),
        window_index(mask_mid, rows // 2, cols // 2),
        window_index(upper, rows // 4, cols // 4),
    ]
    top = top_index(mask_top, row, row_count)
    lists += [top[:2], top[2:]]
    bases, at = [], 0
    for group in lists:
        bases.append(at)
        at += sum(part.shape[0] for part in group)
    index = jnp.concatenate([part for group in lists for part in group], 0)
    tabs = (tables[0], tables[1], tables[2], tables[3], up_table, down_table, near_pair, basis)
    q0, q1, q2, q3, *sends = start_up(field, basis, up_table)
    for step in range(PRODUCTS):
        column, received = exchange(rows, q3, *sends)
        last = step == PRODUCTS - 1
        outs = product(last, tuple(bases), index, field, q0, q1, q2, column, received, tabs)
        field = outs[0]
        if not last:
            q0, q1, q2, q3, *sends = outs[1:]
    return field.reshape(rows, cols, SIDES * LEAF)


def solution(mesh):
    placed = (
        P(("grp", "rhs", "sub"), "br", None),
        P(("grp", "rhs", "sub"), "br", None),
        P(),
        P(),
        P(),
        P(("grp", "rhs", "sub"), "br", None),
        P(("grp", "rhs", "sub"), "br", None),
        P(("grp", "rhs", "sub"), "br", None),
        P("grp", "br", None),
        P("grp", "br", None),
    )
    return jax.shard_map(
        on_device,
        mesh=mesh,
        in_specs=placed,
        out_specs=P(("grp", "rhs", "sub"), "br", None),
        check_vma=False,
    )
```

time: 2060 us -> 199 us (0.10); the launches traced: 2030 us -> 199 us
  other arithmetic: 978 us -> 12.3 us
  local copies, waits for them, and re-layouts: 771 us -> 21.6 us
  starting transfers between devices: 160 us -> 29.5 us
  Pallas kernels: 0 us -> 101 us
  matrix products: 72.4 us -> 0 us
    unnamed x1006 -> x0, other arithmetic: 477 us -> none
    slice x330 -> x0, other arithmetic: 434 us -> none  [the longest x324 426 us: couple_block(): slot_mask[row_par::2, col_par::2, slot_index].astype(coeffs.dtype)]
    slice x363 -> x32, local copies, waits for them, and re-layouts: 362 us -> 1.97 us  [the longest x12 1.01 us: window_index(): kept = slot_mask[row_par::2, col_par::2] != 0]
    squeeze x160 -> x1, local copies, waits for them, and re-layouts: 236 us -> 4.42 us  [on_device(): tables[3]]
    ppermute x54 -> x12, starting transfers between devices: 160 us -> 29.5 us  [shift(): return lax.ppermute(value, axis, pairs)]
    pallas_call x0 -> x4, Pallas kernels: none -> 101 us  [the longest x3 96.2 us: product(): pl.pallas_call(functools.partial(product_kernel, last, sizes), out_shape=...]
    unnamed x1555 -> x61, local copies, waits for them, and re-layouts: 94.1 us -> 0.3 us
    dot_general x75 -> x0, matrix products: 72.4 us -> none  [the longest x48 47.9 us: couple_block(): jnp.einsum('ijsr,rt->ijst', stacked, joined_table, preferred_element_type...]
  transfers between devices with their start and end apart: 54 -> 12, of which waited for: 6 -> 4; matrix products, arithmetic and copies ran while one was open for 83% -> 11% of each run, Pallas kernels for 0% -> 0%
where the time goes in v1:
time: 199 us
  Pallas kernels  101 us (51%)
  starting transfers between devices  29.5 us (15%)
  blocking collectives  23.7 us (12%)
  local copies, waits for them, and re-layouts  21.6 us (11%)
  other arithmetic  12.3 us (6%)
  waiting for transfers between devices  9.7 us (5%)
    pallas_call x3, Pallas kernels, product(): pl.pallas_call(functools.partial(product_kernel, last, sizes), out_shape=...  96.2 us
    ppermute x12, starting transfers between devices, shift(): return lax.ppermute(value, axis, pairs)  29.5 us
    all_gather x3, blocking collectives, exchange(): column = lax.all_gather(wide, ROW_AXES, axis=0, tiled=True)  23.7 us
    concatenate x5, other arithmetic, paired(): return jnp.concatenate([upper, lower], -2)  9.91 us
    ppermute x12, waiting for transfers between devices, shift(): return lax.ppermute(value, axis, pairs)  9.7 us
    reshape x1, local copies, waits for them, and re-layouts, on_device(): tables = paired(coupling.reshape(4, 49, RANK, RANK))  5.79 us
    pallas_call x1, Pallas kernels, start_up(): pl.pallas_call(first_kernel, out_shape=outs, in_specs=[VMEM] * 3, out_spe...  4.93 us
    squeeze x1, local copies, waits for them, and re-layouts, on_device(): tables[3]  4.42 us
  transfers between devices with their start and end apart: 12, of which 4 were waited for; matrix products, arithmetic and copies ran while one was open for 11% of the time, Pallas kernels for 0%

profile of v1, /device:TPU:15, one launch (start us, length us, event | category | flops | bytes accessed | tf_op | source)
XLA Modules:
  0.0 198.8 jit_solution(6967972224366265336)
XLA Ops:
  1.3 4.3 %reshape.408 = bf16[128,64,64]{2,1,0:T(8,128)(2,1)} reshape(bf16[8,16,4096]{2,1,0:T(8,128)(2,1)} %param.36) | data formatting | bytes 2097152 | tf_op jit(solution)/shard_map/reshape | solution.py:407
  5.6 4.8 %fusion.5.basis.refs_17_ = bf16[128,128,128]{2,1,0:T(8,128)(2,1)} fusion(bf16[128,64,64]{2,1,0:T(8,128)(2,1)} %reshape.408), kind=kLoop, calls=%fused_computation.9 | loop fusion | flops 16777216 | bytes 5242880 | tf_op jit(solution)/shard_map/concatenate | solution.py:43
  10.5 4.9 %shard_map.325 = (bf16[8,16,16,128]{3,2,1,0:T(8,128)(2,1)S(1)}, bf16[4,8,16,128]{3,2,1,0:T(8,128)(2,1)S(1)}, bf16[2,4,16,128]{3,2,1,0:T(8,128)(2,1)S(1)}, bf16[1...) custom-call(bf16[8,16,16,128]{3,2,1,0:T(8,128)(2,1)S(1)} %bitcast.32, ...), custom_call_target="tpu_custom_call" | custom-call | tf_op jit(solution)/shard_map/pallas_call | solution.py:335
  15.5 3.2 %collective-permute-start = (bf16[38,16,128]{2,1,0:T(8,128)(2,1)S(1)}, bf16[38,16,128]{2,1,0:T(8,128)(2,1)S(1)}, u32[]{:S(2)}, u32[]{:S(2)}) collective-permute-start(bf16[38,16,128]{2,1,0:T(8,128)(2,1)S(1)} %get-tuple-element.35), channel_id=1, source_target_pairs={{0,4},{4,8},{8,12},{1,5},{5,9},{9,13},{2,6},{6,10},{10,14},{3,7},{... | collective-permute-start | bytes 466952 | tf_op jit(solution)/shard_map/ppermute | solution.py:380
  18.7 2.1 %collective-permute-start.1 = (bf16[38,16,128]{2,1,0:T(8,128)(2,1)S(1)}, bf16[38,16,128]{2,1,0:T(8,128)(2,1)S(1)}, u32[]{:S(2)}, u32[]{:S(2)}) collective-permute-start(bf16[38,16,128]{2,1,0:T(8,128)(2,1)S(1)} %get-tuple-element.36), channel_id=1, source_target_pairs={{4,0},{8,4},{12,8},{5,1},{9,5},{13,9},{6,2},{10,6},{14,10},{7,3},{... | collective-permute-start | bytes 466952 | tf_op jit(solution)/shard_map/ppermute | solution.py:380
  22.0 5.8 %reshape.410 = bf16[4,49,64,64]{3,2,0,1:T(8,128)(2,1)} reshape(bf16[4,49,4096]{2,0,1:T(4,128)(2,1)} %param.38) | data formatting | bytes 3211264 | tf_op jit(solution)/shard_map/reshape | solution.py:408
  27.8 4.7 %fusion.4 = bf16[4,49,128,128]{3,2,1,0:T(8,128)(2,1)S(1)} fusion(bf16[4,49,64,64]{3,2,0,1:T(8,128)(2,1)} %reshape.410), kind=kLoop, calls=%fused_computation.8 | loop fusion | flops 25690112 | bytes 8028160 | tf_op jit(solution)/shard_map/concatenate | solution.py:43
  32.8 4.4 %slice_bitcast_fusion = (bf16[49,128,128]{2,1,0:T(8,128)(2,1)}, bf16[49,128,128]{2,1,0:T(8,128)(2,1)}, bf16[49,128,128]{2,1,0:T(8,128)(2,1)}, bf16[49,128,128]{2,1,0:T(8,128)(2,1)}) fusion(bf16[4,49,128,128]{3,2,1,0:T(8,128)(2,1)S(1)} %fusion.4), kind=kLoop, calls=%fused_computation.10 | loop fusion | bytes 12845056 | tf_op jit(solution)/shard_map/squeeze | solution.py:427
  39.4 3.2 %collective-permute-start.3 = (bf16[98,16,128]{2,1,0:T(8,128)(2,1)}, bf16[98,16,128]{2,1,0:T(8,128)(2,1)S(1)}, u32[]{:S(2)}, u32[]{:S(2)}) collective-permute-start(bf16[98,16,128]{2,1,0:T(8,128)(2,1)} %pad_maximum_fusion.1), channel_id=1, source_target_pairs={{1,0},{2,1},{3,2},{5,4},{6,5},{7,6},{9,8},{10,9},{11,10},{13,12},{... | collective-permute-start | bytes 1204232 | tf_op jit(solution)/shard_map/ppermute | solution.py:380
  47.9 6.5 %all_gather.9.refs_5_ = bf16[24,16,128]{2,1,0:T(8,128)(2,1)S(1)} all-gather(bf16[6,16,128]{2,1,0:T(8,128)(2,1)S(1)} %pad_maximum_fusion.6), channel_id=1, replica_groups=mesh['grp'=2,'br'=4,'rhs'=2,'sub'=2] {'rhs','sub'}, dimensions={0}, use_global_device_ids=true | all-gather | bytes 122880 | tf_op jit(solution)/shard_map/all_gather | solution.py:395
  54.4 33.1 %shard_map.326 = (bf16[8,16,16,128]{3,2,1,0:T(8,128)(2,1)S(1)}, bf16[8,16,16,128]{3,2,1,0:T(8,128)(2,1)S(1)}, bf16[4,8,16,128]{3,2,1,0:T(8,128)(2,1)S(1)}, bf16[...) custom-call(s32[5796]{0:T(1024)S(1)} %concatenate.75.refs_0_, ...), custom_call_target="tpu_custom_call" | custom-call | tf_op jit(solution)/shard_map/pallas_call | solution.py:354
  87.5 3.2 %collective-permute-start.4 = (bf16[38,16,128]{2,1,0:T(8,128)(2,1)S(1)}, bf16[38,16,128]{2,1,0:T(8,128)(2,1)S(1)}, u32[]{:S(2)}, u32[]{:S(2)}) collective-permute-start(bf16[38,16,128]{2,1,0:T(8,128)(2,1)S(1)} %get-tuple-element.44), channel_id=1, source_target_pairs={{0,4},{4,8},{8,12},{1,5},{5,9},{9,13},{2,6},{6,10},{10,14},{3,7},{... | collective-permute-start | bytes 466952 | tf_op jit(solution)/shard_map/ppermute | solution.py:380
  90.7 2.1 %collective-permute-start.5 = (bf16[38,16,128]{2,1,0:T(8,128)(2,1)S(1)}, bf16[38,16,128]{2,1,0:T(8,128)(2,1)S(1)}, u32[]{:S(2)}, u32[]{:S(2)}) collective-permute-start(bf16[38,16,128]{2,1,0:T(8,128)(2,1)S(1)} %get-tuple-element.45), channel_id=1, source_target_pairs={{4,0},{8,4},{12,8},{5,1},{9,5},{13,9},{6,2},{10,6},{14,10},{7,3},{... | collective-permute-start | bytes 466952 | tf_op jit(solution)/shard_map/ppermute | solution.py:380
  92.8 2.1 %collective-permute-done.4.refs_6_ = bf16[38,16,128]{2,1,0:T(8,128)(2,1)S(1)} collective-permute-done((bf16[38,16,128]{2,1,0:T(8,128)(2,1)S(1)}, bf16[38,16,128]{2,1,0:T(8,128)(2,1)S(1)}, u32[]{:S(2)}, u32[]{:S(2)}) %collective-permute-start.4) | collective-permute-done | bytes 155680 | tf_op jit(solution)/shard_map/ppermute | solution.py:380
  94.9 2.9 %collective-permute-done.5.refs_7_ = bf16[38,16,128]{2,1,0:T(8,128)(2,1)S(1)} collective-permute-done((bf16[38,16,128]{2,1,0:T(8,128)(2,1)S(1)}, bf16[38,16,128]{2,1,0:T(8,128)(2,1)S(1)}, u32[]{:S(2)}, u32[]{:S(2)}) %collective-permute-start.5) | collective-permute-done | bytes 155680 | tf_op jit(solution)/shard_map/ppermute | solution.py:380
  97.8 3.2 %collective-permute-start.7 = (bf16[98,16,128]{2,1,0:T(8,128)(2,1)S(1)}, bf16[98,16,128]{2,1,0:T(8,128)(2,1)S(1)}, u32[]{:S(2)}, u32[]{:S(2)}) collective-permute-start(bf16[98,16,128]{2,1,0:T(8,128)(2,1)S(1)} %pad_maximum_fusion.3), channel_id=1, source_target_pairs={{1,0},{2,1},{3,2},{5,4},{6,5},{7,6},{9,8},{10,9},{11,10},{13,12},{... | collective-permute-start | bytes 1204232 | tf_op jit(solution)/shard_map/ppermute | solution.py:380
  102.4 8.6 %all_gather.10.refs_5_ = bf16[24,16,128]{2,1,0:T(8,128)(2,1)S(1)} all-gather(bf16[6,16,128]{2,1,0:T(8,128)(2,1)S(1)} %pad_maximum_fusion.7), channel_id=1, replica_groups=mesh['grp'=2,'br'=4,'rhs'=2,'sub'=2] {'rhs','sub'}, dimensions={0}, use_global_device_ids=true | all-gather | bytes 122880 | tf_op jit(solution)/shard_map/all_gather | solution.py:395
  111.0 33.2 %shard_map.327 = (bf16[8,16,16,128]{3,2,1,0:T(8,128)(2,1)S(1)}, bf16[8,16,16,128]{3,2,1,0:T(8,128)(2,1)S(1)}, bf16[4,8,16,128]{3,2,1,0:T(8,128)(2,1)S(1)}, bf16[...) custom-call(s32[5796]{0:T(1024)S(1)} %concatenate.75.refs_0_, ...), custom_call_target="tpu_custom_call" | custom-call | tf_op jit(solution)/shard_map/pallas_call | solution.py:354
  144.2 3.2 %collective-permute-start.8 = (bf16[38,16,128]{2,1,0:T(8,128)(2,1)S(1)}, bf16[38,16,128]{2,1,0:T(8,128)(2,1)S(1)}, u32[]{:S(2)}, u32[]{:S(2)}) collective-permute-start(bf16[38,16,128]{2,1,0:T(8,128)(2,1)S(1)} %get-tuple-element.53), channel_id=1, source_target_pairs={{0,4},{4,8},{8,12},{1,5},{5,9},{9,13},{2,6},{6,10},{10,14},{3,7},{... | collective-permute-start | bytes 466952 | tf_op jit(solution)/shard_map/ppermute | solution.py:380
  147.4 2.1 %collective-permute-start.9 = (bf16[38,16,128]{2,1,0:T(8,128)(2,1)S(1)}, bf16[38,16,128]{2,1,0:T(8,128)(2,1)S(1)}, u32[]{:S(2)}, u32[]{:S(2)}) collective-permute-start(bf16[38,16,128]{2,1,0:T(8,128)(2,1)S(1)} %get-tuple-element.54), channel_id=1, source_target_pairs={{4,0},{8,4},{12,8},{5,1},{9,5},{13,9},{6,2},{10,6},{14,10},{7,3},{... | collective-permute-start | bytes 466952 | tf_op jit(solution)/shard_map/ppermute | solution.py:380
  151.4 2.9 %collective-permute-done.9.refs_7_ = bf16[38,16,128]{2,1,0:T(8,128)(2,1)S(1)} collective-permute-done((bf16[38,16,128]{2,1,0:T(8,128)(2,1)S(1)}, bf16[38,16,128]{2,1,0:T(8,128)(2,1)S(1)}, u32[]{:S(2)}, u32[]{:S(2)}) %collective-permute-start.9) | collective-permute-done | bytes 155680 | tf_op jit(solution)/shard_map/ppermute | solution.py:380
  154.4 3.4 %collective-permute-start.11 = (bf16[98,16,128]{2,1,0:T(8,128)(2,1)S(1)}, bf16[98,16,128]{2,1,0:T(8,128)(2,1)S(1)}, u32[]{:S(2)}, u32[]{:S(2)}) collective-permute-start(bf16[98,16,128]{2,1,0:T(8,128)(2,1)S(1)} %pad_maximum_fusion.5), channel_id=1, source_target_pairs={{1,0},{2,1},{3,2},{5,4},{6,5},{7,6},{9,8},{10,9},{11,10},{13,12},{... | collective-permute-start | bytes 1204232 | tf_op jit(solution)/shard_map/ppermute | solution.py:380
  159.2 8.6 %all_gather.11.refs_5_ = bf16[24,16,128]{2,1,0:T(8,128)(2,1)S(1)} all-gather(bf16[6,16,128]{2,1,0:T(8,128)(2,1)S(1)} %pad_maximum_fusion.8), channel_id=1, replica_groups=mesh['grp'=2,'br'=4,'rhs'=2,'sub'=2] {'rhs','sub'}, dimensions={0}, use_global_device_ids=true | all-gather | bytes 122880 | tf_op jit(solution)/shard_map/all_gather | solution.py:395
  167.8 29.9 %shard_map.328 = bf16[8,16,16,128]{3,2,1,0:T(8,128)(2,1)S(1)} custom-call(s32[5796]{0:T(1024)S(1)} %concatenate.75.refs_0_, bf16[8,16,16,128]{3,2,1,0:T(8,128)(2,1)S(1)} %get-tuple-element.48.refs_1_, bf16[8,16,16,128]{3,2,1,0:T(8,128)(2,1)S(1)} %get-tuple-element.49.refs_2_, bf16[4,8,16,128]{3,2,1,0:T(8,128)(2,1)S(1)} %get-tuple-element.50.refs_3_, ...), custom_call_target="tpu_custom_call" | custom-call | tf_op jit(solution)/shard_map/pallas_call | solution.py:354
  (155 shorter events, 15.5 us)
Async XLA Ops:
  0.0 20.8 %copy-start = (s32[8,4,27]{2,1,0:T(4,128)S(1)}, s32[8,4,27]{2,1,0:T(4,128)}, u32[]{:S(2)}) copy-start(s32[8,4,27]{2,1,0:T(4,128)} %param.43) | copy-start | bytes 10372
  1.3 9.1 %copy-start.2 = (bf16[8,16,2048]{2,1,0:T(8,128)(2,1)S(1)}, bf16[8,16,2048]{2,1,0:T(8,128)(2,1)}, u32[]{:S(2)}) copy-start(bf16[8,16,2048]{2,1,0:T(8,128)(2,1)} %param.35) | copy-start | bytes 1572868
  10.4 10.5 %copy-start.4 = (s32[8,16,27]{2,1,0:T(8,128)S(1)}, s32[8,16,27]{2,1,0:T(8,128)}, u32[]{:S(2)}) copy-start(s32[8,16,27]{2,1,0:T(8,128)} %param.41) | copy-start | bytes 41476
  10.4 11.1 %copy-start.6 = (s32[4,8,27]{2,1,0:T(8,128)S(1)}, s32[4,8,27]{2,1,0:T(8,128)}, u32[]{:S(2)}) copy-start(s32[4,8,27]{2,1,0:T(8,128)} %param.42) | copy-start | bytes 10372
  15.5 23.1 %collective-permute-start = (bf16[38,16,128]{2,1,0:T(8,128)(2,1)S(1)}, bf16[38,16,128]{2,1,0:T(8,128)(2,1)S(1)}, u32[]{:S(2)}, u32[]{:S(2)}) collective-permute-start(bf16[38,16,128]{2,1,0:T(8,128)(2,1)S(1)} %get-tuple-element.35), channel_id=1, source_target_pairs={{0,4},{4,8},{8,12},{1,5},{5,9},{9,13},{2,6},{6,10},{10,14},{3,7},{... | collective-permute-start | bytes 466952 | tf_op jit(solution)/shard_map/ppermute | solution.py:380
  18.7 19.9 %collective-permute-start.1 = (bf16[38,16,128]{2,1,0:T(8,128)(2,1)S(1)}, bf16[38,16,128]{2,1,0:T(8,128)(2,1)S(1)}, u32[]{:S(2)}, u32[]{:S(2)}) collective-permute-start(bf16[38,16,128]{2,1,0:T(8,128)(2,1)S(1)} %get-tuple-element.36), channel_id=1, source_target_pairs={{4,0},{8,4},{12,8},{5,1},{9,5},{13,9},{6,2},{10,6},{14,10},{7,3},{... | collective-permute-start | bytes 466952 | tf_op jit(solution)/shard_map/ppermute | solution.py:380
  32.7 5.8 %copy-start.20 = (s32[27]{0:T(128)S(1)}, s32[27]{0:T(128)}, u32[]{:S(2)}) copy-start(s32[27]{0:T(128)} %constant.118.clone) | copy-start | bytes 328
  32.7 5.8 %copy-start.21 = (s32[27]{0:T(128)S(1)}, s32[27]{0:T(128)}, u32[]{:S(2)}) copy-start(s32[27]{0:T(128)} %constant.119.clone) | copy-start | bytes 328
  32.8 11.9 %copy-start.16 = (s32[27]{0:T(128)S(1)}, s32[27]{0:T(128)}, u32[]{:S(2)}) copy-start(s32[27]{0:T(128)} %constant.122.clone) | copy-start | bytes 328
  32.8 11.9 %copy-start.17 = (s32[27]{0:T(128)S(1)}, s32[27]{0:T(128)}, u32[]{:S(2)}) copy-start(s32[27]{0:T(128)} %constant.123.clone) | copy-start | bytes 328
  32.8 11.9 %copy-start.18 = (s32[27]{0:T(128)S(1)}, s32[27]{0:T(128)}, u32[]{:S(2)}) copy-start(s32[27]{0:T(128)} %constant.126.clone) | copy-start | bytes 328
  32.8 11.9 %copy-start.19 = (s32[27]{0:T(128)S(1)}, s32[27]{0:T(128)}, u32[]{:S(2)}) copy-start(s32[27]{0:T(128)} %constant.127.clone) | copy-start | bytes 328
  32.8 14.5 %copy-start.3 = (bf16[9,4096]{1,0:T(8,128)(2,1)S(1)}, bf16[9,4096]{1,0:T(8,128)(2,1)}, u32[]{:S(2)}) copy-start(bf16[9,4096]{1,0:T(8,128)(2,1)} %param.39) | copy-start | bytes 221188
  39.4 15.0 %collective-permute-start.3 = (bf16[98,16,128]{2,1,0:T(8,128)(2,1)}, bf16[98,16,128]{2,1,0:T(8,128)(2,1)S(1)}, u32[]{:S(2)}, u32[]{:S(2)}) collective-permute-start(bf16[98,16,128]{2,1,0:T(8,128)(2,1)} %pad_maximum_fusion.1), channel_id=1, source_target_pairs={{1,0},{2,1},{3,2},{5,4},{6,5},{7,6},{9,8},{10,9},{11,10},{13,12},{... | collective-permute-start | bytes 1204232 | tf_op jit(solution)/shard_map/ppermute | solution.py:380
  43.4 11.0 %collective-permute-start.2 = (bf16[98,16,128]{2,1,0:T(8,128)(2,1)}, bf16[98,16,128]{2,1,0:T(8,128)(2,1)S(1)}, u32[]{:S(2)}, u32[]{:S(2)}) collective-permute-start(bf16[98,16,128]{2,1,0:T(8,128)(2,1)} %pad_maximum_fusion), channel_id=1, source_target_pairs={{0,1},{1,2},{2,3},{4,5},{5,6},{6,7},{8,9},{9,10},{10,11},{12,13},{... | collective-permute-start | bytes 1204232 | tf_op jit(solution)/shard_map/ppermute | solution.py:380
  87.5 7.4 %collective-permute-start.4 = (bf16[38,16,128]{2,1,0:T(8,128)(2,1)S(1)}, bf16[38,16,128]{2,1,0:T(8,128)(2,1)S(1)}, u32[]{:S(2)}, u32[]{:S(2)}) collective-permute-start(bf16[38,16,128]{2,1,0:T(8,128)(2,1)S(1)} %get-tuple-element.44), channel_id=1, source_target_pairs={{0,4},{4,8},{8,12},{1,5},{5,9},{9,13},{2,6},{6,10},{10,14},{3,7},{... | collective-permute-start | bytes 466952 | tf_op jit(solution)/shard_map/ppermute | solution.py:380
  90.7 7.1 %collective-permute-start.5 = (bf16[38,16,128]{2,1,0:T(8,128)(2,1)S(1)}, bf16[38,16,128]{2,1,0:T(8,128)(2,1)S(1)}, u32[]{:S(2)}, u32[]{:S(2)}) collective-permute-start(bf16[38,16,128]{2,1,0:T(8,128)(2,1)S(1)} %get-tuple-element.45), channel_id=1, source_target_pairs={{4,0},{8,4},{12,8},{5,1},{9,5},{13,9},{6,2},{10,6},{14,10},{7,3},{... | collective-permute-start | bytes 466952 | tf_op jit(solution)/shard_map/ppermute | solution.py:380
  97.8 13.2 %collective-permute-start.7 = (bf16[98,16,128]{2,1,0:T(8,128)(2,1)S(1)}, bf16[98,16,128]{2,1,0:T(8,128)(2,1)S(1)}, u32[]{:S(2)}, u32[]{:S(2)}) collective-permute-start(bf16[98,16,128]{2,1,0:T(8,128)(2,1)S(1)} %pad_maximum_fusion.3), channel_id=1, source_target_pairs={{1,0},{2,1},{3,2},{5,4},{6,5},{7,6},{9,8},{10,9},{11,10},{13,12},{... | collective-permute-start | bytes 1204232 | tf_op jit(solution)/shard_map/ppermute | solution.py:380
  101.1 9.9 %collective-permute-start.6 = (bf16[98,16,128]{2,1,0:T(8,128)(2,1)S(1)}, bf16[98,16,128]{2,1,0:T(8,128)(2,1)S(1)}, u32[]{:S(2)}, u32[]{:S(2)}) collective-permute-start(bf16[98,16,128]{2,1,0:T(8,128)(2,1)S(1)} %pad_maximum_fusion.2), channel_id=1, source_target_pairs={{0,1},{1,2},{2,3},{4,5},{5,6},{6,7},{8,9},{9,10},{10,11},{12,13},{... | collective-permute-start | bytes 1204232 | tf_op jit(solution)/shard_map/ppermute | solution.py:380
  111.0 56.8 %copy-start.1 = (bf16[49,128,128]{2,1,0:T(8,128)(2,1)S(1)}, bf16[49,128,128]{2,1,0:T(8,128)(2,1)}, u32[]{:S(2)}) copy-start(bf16[49,128,128]{2,1,0:T(8,128)(2,1)} %get-tuple-element.60.refs_10_) | copy-start | bytes 4816900
  144.2 7.2 %collective-permute-start.8 = (bf16[38,16,128]{2,1,0:T(8,128)(2,1)S(1)}, bf16[38,16,128]{2,1,0:T(8,128)(2,1)S(1)}, u32[]{:S(2)}, u32[]{:S(2)}) collective-permute-start(bf16[38,16,128]{2,1,0:T(8,128)(2,1)S(1)} %get-tuple-element.53), channel_id=1, source_target_pairs={{0,4},{4,8},{8,12},{1,5},{5,9},{9,13},{2,6},{6,10},{10,14},{3,7},{... | collective-permute-start | bytes 466952 | tf_op jit(solution)/shard_map/ppermute | solution.py:380
  147.4 6.8 %collective-permute-start.9 = (bf16[38,16,128]{2,1,0:T(8,128)(2,1)S(1)}, bf16[38,16,128]{2,1,0:T(8,128)(2,1)S(1)}, u32[]{:S(2)}, u32[]{:S(2)}) collective-permute-start(bf16[38,16,128]{2,1,0:T(8,128)(2,1)S(1)} %get-tuple-element.54), channel_id=1, source_target_pairs={{4,0},{8,4},{12,8},{5,1},{9,5},{13,9},{6,2},{10,6},{14,10},{7,3},{... | collective-permute-start | bytes 466952 | tf_op jit(solution)/shard_map/ppermute | solution.py:380
  154.4 13.4 %collective-permute-start.11 = (bf16[98,16,128]{2,1,0:T(8,128)(2,1)S(1)}, bf16[98,16,128]{2,1,0:T(8,128)(2,1)S(1)}, u32[]{:S(2)}, u32[]{:S(2)}) collective-permute-start(bf16[98,16,128]{2,1,0:T(8,128)(2,1)S(1)} %pad_maximum_fusion.5), channel_id=1, source_target_pairs={{1,0},{2,1},{3,2},{5,4},{6,5},{7,6},{9,8},{10,9},{11,10},{13,12},{... | collective-permute-start | bytes 1204232 | tf_op jit(solution)/shard_map/ppermute | solution.py:380
  157.9 9.9 %collective-permute-start.10 = (bf16[98,16,128]{2,1,0:T(8,128)(2,1)S(1)}, bf16[98,16,128]{2,1,0:T(8,128)(2,1)S(1)}, u32[]{:S(2)}, u32[]{:S(2)}) collective-permute-start(bf16[98,16,128]{2,1,0:T(8,128)(2,1)S(1)} %pad_maximum_fusion.4), channel_id=1, source_target_pairs={{0,1},{1,2},{2,3},{4,5},{5,6},{6,7},{8,9},{9,10},{10,11},{12,13},{... | collective-permute-start | bytes 1204232 | tf_op jit(solution)/shard_map/ppermute | solution.py:380
  (18 other events, 102.1 us)

commit v2 on v1

v2 whole, which is shorter than its diff:
```python
import functools

import jax
import jax.numpy as jnp
from jax import lax
from jax.experimental import pallas as pl
from jax.experimental.pallas import tpu as pltpu
from jax.sharding import PartitionSpec as P

LEAF = 64
RANK = 64
SIDES = 32
PRODUCTS = 3
PAIRS = SIDES // 2
WIDE = 2 * RANK
SLOTS = 27
ROW_AXES = ("rhs", "sub")
UP_AT = 4 * 49
NEAR_AT = UP_AT + 12
DOWN_AT = NEAR_AT + 10
BF16 = jnp.bfloat16
F32 = jnp.float32


def window_slots(row_par, col_par):
    slots = []
    for a in range(6):
        for b in range(6):
            if abs(a - 2 - row_par) <= 1 and abs(b - 2 - col_par) <= 1:
                continue
            slots.append((a, b))
    return slots


def offset_index(slot, row_par, col_par):
    return 7 * (slot[0] + 1 - row_par) + slot[1] + 1 - col_par


CLASSES = [(row_par, col_par) for row_par in range(2) for col_par in range(2)]


def top_index(mask_top, row, count, place_row):
    parity = row % 2
    mask_row = lax.dynamic_slice_in_dim(mask_top, row, 1, 0)[0]
    place = [2, 3, 0, 1, 4, 5]
    tiles, tables = [], []
    for col_par in range(2):
        lists = [window_slots(row_par, col_par) for row_par in range(2)]
        a, b, o = [
            jnp.where(parity == 0, jnp.asarray(even, jnp.int32), jnp.asarray(odd, jnp.int32))
            for even, odd in (
                ([s[0] for s in lists[0]], [s[0] for s in lists[1]]),
                ([place[s[1]] for s in lists[0]], [place[s[1]] for s in lists[1]]),
                (
                    [offset_index(s, 0, col_par) for s in lists[0]],
                    [offset_index(s, 1, col_par) for s in lists[1]],
                ),
            )
        ]
        source = row - parity + a - 2
        kept = (mask_row[col_par] != 0) & (source >= 0) & (source < count)
        tiles.append(jnp.where(kept, place_row(source) * 6 + b, 6 * count))
        tables.append(o)
    return tiles + tables


def dot(a, b):
    return jnp.dot(a, b, preferred_element_type=F32)


def dot_t(a, b):
    return lax.dot_general(a, b, (((1,), (1,)), ((), ())), preferred_element_type=F32)


def halves(ref):
    rows, cols = ref.shape[0], ref.shape[1]
    return ref.reshape(rows // 2, 2, cols // 2, 2, PAIRS, WIDE)


def tiles_of(value):
    return value.reshape(-1, WIDE)


def climb(child, parent, table, first):
    rows, cols = parent.shape[0], parent.shape[1]
    total = None
    for c, (a, b) in enumerate(CLASSES):
        block = tiles_of(halves(child)[:, a, :, b])
        part = dot(block, table[first + c])
        total = part if total is None else total + part
    parent[...] = total.astype(BF16).reshape(rows, cols, PAIRS, WIDE)


def upward_pass(field, basis, table, first, q0, q1, q2, q3, send_l, send_r, send_u, send_d):
    rows, cols = field.shape[0], field.shape[1]

    def leaf_row(i, carry):
        for j in range(cols):
            q0[i, j] = dot(field[i, j], basis[i * cols + j]).astype(BF16)
        return carry

    lax.fori_loop(0, rows, leaf_row, 0)
    climb(q0, q1, table, first + 0)
    climb(q1, q2, table, first + 4)
    climb(q2, q3, table, first + 8)
    for ref, side in ((send_l, 0), (send_r, 1)):
        at = 0
        for source, first, last, width in col_message(rows):
            level = (q0, q1, q2, q3, field)[source]
            low = 0 if side == 0 else level.shape[1] - width
            for r in range(first, last):
                ref[at : at + width] = level[r, low : low + width]
                at += width
    for ref, side in ((send_u, 0), (send_d, 1)):
        at = 0
        for level, width in ((q0, 2), (field, 1), (q1, 2), (q2, 2)):
            low = 0 if side == 0 else level.shape[0] - width
            for r in range(low, low + width):
                ref[at : at + level.shape[1]] = level[r]
                at += level.shape[1]


def col_message(rows):
    return [
        (0, 2, rows - 2, 2),
        (4, 1, rows - 1, 1),
        (0, 0, 2, 2),
        (4, 0, 1, 1),
        (1, 0, 2, 2),
        (2, 0, rows // 4, 2),
        (0, rows - 2, rows, 2),
        (4, rows - 1, rows, 1),
        (1, rows // 2 - 2, rows // 2, 2),
        (3, 0, rows // 8, 2),
    ]


def message_sizes(rows):
    counts = [(last - first) * width for _, first, last, width in col_message(rows)]
    start = sum(counts[:2])
    up = (start, start + sum(counts[2:6]))
    down = (start + sum(counts[2:5]), start + sum(counts[2:9]))
    return counts, up, down


def fill_windows(own, recv_l, recv_r, recv_u, recv_d, pads):
    q0, q1, q2, field = own
    p0, p1, p2, pf = pads
    rows = q0.shape[0]

    def place(level):
        ref, halo = {0: (p0, 2), 1: (p1, 2), 2: (p2, 2), 4: (pf, 1)}[level]
        source = {0: q0, 1: q1, 2: q2, 4: field}[level]
        return ref, halo, source.shape[0], source.shape[1]

    for level, source in ((0, q0), (1, q1), (2, q2), (4, field)):
        ref, halo, level_rows, level_cols = place(level)
        width = level_cols + 2 * halo
        for r in range(level_rows):
            start = (r + halo) * width + halo
            ref[start : start + level_cols] = source[r]
    for recv, side in ((recv_l, 0), (recv_r, 1)):
        at = 0
        for level, first, last, count in col_message(rows)[:-1]:
            ref, halo, level_rows, level_cols = place(level)
            width = level_cols + 2 * halo
            for r in range(first, last):
                start = (r + halo) * width + (0 if side == 0 else halo + level_cols)
                ref[start : start + count] = recv[at : at + count]
                at += count
    for recv, side in ((recv_u, 0), (recv_d, 1)):
        at = 0
        for level in (0, 4, 1, 2):
            ref, halo, level_rows, level_cols = place(level)
            width = level_cols + 2 * halo
            for r in range(halo):
                row = r if side == 0 else halo + level_rows + r
                start = row * width + halo
                ref[start : start + level_cols] = recv[at : at + level_cols]
                at += level_cols
        corner = (2, 0, 4, 1) if side == 0 else (0, 4, 1, 2)
        for edge in range(2):
            for level in corner:
                ref, halo, level_rows, level_cols = place(level)
                width = level_cols + 2 * halo
                for r in range(halo):
                    row = r if side == 0 else halo + level_rows + r
                    start = row * width + (0 if edge == 0 else halo + level_cols)
                    ref[start : start + halo] = recv[at : at + halo]
                    at += halo


def contract(lhs, count, tables, chunk=4):
    total = None
    for start in range(0, len(tables), chunk):
        group = tables[start : start + chunk]
        block = lhs[0:count, :, start * WIDE : (start + len(group)) * WIDE]
        weights = jnp.concatenate([read() for read in group], 0)
        part = dot(block.reshape(count * PAIRS, len(group) * WIDE), weights)
        total = part if total is None else total + part
    return total


def masked(tiles, words, bit):
    parts = []
    for n, (i, j) in enumerate(words[1]):
        kept = jnp.bitwise_and(words[0][i, j : j + 1, :], jnp.int32(1 << bit)) != 0
        kept = jnp.broadcast_to(kept, (PAIRS, WIDE))
        parts.append(jnp.where(kept, tiles[n], jnp.zeros((), BF16)))
    return jnp.concatenate(parts, 0)


def windows_dot(reads, words, table, extra=None):
    total = None
    for start in range(0, len(reads), 2):
        group = list(enumerate(reads))[start : start + 2]
        blocks = [masked(read(), words, k) for k, (read, _) in group]
        weights = [table[at] for _, (_, at) in group]
        if extra is not None and len(group) == 1:
            blocks.append(extra[0])
            weights.append(extra[1])
        part = dot(jnp.concatenate(blocks, 1), jnp.concatenate(weights, 0))
        total = part if total is None else total + part
    return total


def far_level(level, words, padded, table, parent, out):
    rows, cols = out.shape[0], out.shape[1]
    half_rows, half_cols = rows // 2, cols // 2
    grid = padded.reshape(half_rows + 2, 2, half_cols + 2, 2, PAIRS, WIDE)
    for c, (row_par, col_par) in enumerate(CLASSES):
        spots = [
            (2 * i + row_par, 2 * j + col_par) for i in range(half_rows) for j in range(half_cols)
        ]

        def read(a, b):
            value = grid[a // 2 : a // 2 + half_rows, a % 2, b // 2 : b // 2 + half_cols, b % 2]
            return value.reshape(half_rows * half_cols, PAIRS, WIDE)

        reads = [
            (
                functools.partial(read, slot[0], slot[1]),
                49 * level + offset_index(slot, row_par, col_par),
            )
            for slot in window_slots(row_par, col_par)
        ]
        extra = (tiles_of(parent[...]), table[DOWN_AT + 4 * level + c])
        total = windows_dot(reads, (words, spots), table, extra)
        halves(out)[:, row_par, :, col_par] = total.astype(BF16).reshape(
            half_rows, half_cols, PAIRS, WIDE
        )


def product_kernel(last, row_tiles, *refs):
    (
        index, words_near, words0, words1, words2, field, q0, q1, q2, column,
        recv_l, recv_r, recv_u, recv_d, table, basis,
    ) = refs[:16]
    outs = refs[16 : 17 if last else 25]
    p0, p1, p2, p3, pf, g0, g1, g2, g3, near, lhs = refs[17 if last else 25 :]
    rows, cols = field.shape[0], field.shape[1]
    count = column.shape[0]
    fill_windows((q0, q1, q2, field), recv_l, recv_r, recv_u, recv_d, (p0, p1, p2, pf))
    p3[0:count] = column[...]
    p3[count] = jnp.zeros((PAIRS, WIDE), BF16)
    for j in range(2):
        for k in range(SLOTS):
            lhs[0, :, k * WIDE : (k + 1) * WIDE] = p3[index[j * SLOTS + k]]
        reads = [
            functools.partial(lambda k: table[3 * 49 + index[k]], (2 + j) * SLOTS + k)
            for k in range(SLOTS)
        ]
        g3[0, j] = contract(lhs, 1, reads).astype(BF16)
    far_level(2, words2, p2, table, g3, g2)
    far_level(1, words1, p1, table, g2, g1)
    far_level(0, words0, p0, table, g1, g0)
    grid = pf.reshape(rows + 2, cols + 2, PAIRS, WIDE)
    for top in range(0, rows, row_tiles):

        def read(u, v):
            value = grid[top + u : top + u + row_tiles, v : v + cols]
            return value.reshape(row_tiles * cols, PAIRS, WIDE)

        spots = [(top + i, j) for i in range(row_tiles) for j in range(cols)]
        reads = [
            (functools.partial(read, u, v), NEAR_AT + 3 * u + v) for u in range(3) for v in range(3)
        ]
        total = windows_dot(reads, (words_near, spots), table)
        near[top : top + row_tiles] = total.reshape(row_tiles, cols, PAIRS, WIDE)
    result = outs[0]

    def leaf_row(i, carry):
        for j in range(cols):
            far = dot_t(g0[i, j], basis[i * cols + j])
            result[i, j] = (near[i, j] + far).astype(BF16)
        return carry

    lax.fori_loop(0, rows, leaf_row, 0)
    if not last:
        upward_pass(result, basis, table, UP_AT, *outs[1:])


def half_lanes(rows):
    return lax.broadcasted_iota(jnp.int32, (rows, WIDE), 1) < WIDE // 2


def expand_pair(first, second, order):
    low = half_lanes(RANK // 2)
    one, two = first.astype(F32), second.astype(F32)
    upper = jnp.where(low, one, pltpu.roll(two, WIDE // 2, 1))
    lower = jnp.where(low, pltpu.roll(one, WIDE // 2, 1), two)
    both = dot(order, jnp.concatenate([upper, lower], 0).astype(BF16))
    turned = pltpu.roll(both, WIDE // 2, 1)
    low = half_lanes(RANK)
    zero = jnp.zeros((), F32)
    blocks = [
        (jnp.where(low, both, zero), jnp.where(low, zero, turned)),
        (jnp.where(low, turned, zero), jnp.where(low, zero, both)),
    ]
    return [jnp.concatenate(pair, 0) for pair in blocks]


def row_order():
    to = lax.broadcasted_iota(jnp.int32, (RANK, RANK), 0)
    source = lax.broadcasted_iota(jnp.int32, (RANK, RANK), 1)
    return (source == (to % 2) * (RANK // 2) + to // 2).astype(F32).astype(BF16)


def expand(packed, out, count, unroll):
    order = row_order()

    def some(n, carry):
        for k in range(unroll):
            at = 2 * (n * unroll + k)
            one, two = expand_pair(packed[at], packed[at + 1], order)
            out[at] = one.astype(BF16)
            out[at + 1] = two.astype(BF16)
        return carry

    steps = count // 2 // unroll
    lax.fori_loop(0, steps, some, 0)
    for at in range(2 * unroll * steps, count, 2):
        one, two = expand_pair(packed[at], packed[at + 1], order)
        out[at] = one.astype(BF16)
        out[at + 1] = two.astype(BF16)


def first_kernel(field, packed_basis, packed_up, basis, *rest):
    outs, up_table = rest[:-1], rest[-1]
    expand(packed_basis, basis, packed_basis.shape[0], 8)
    expand(packed_up, up_table, packed_up.shape[0], 6)
    upward_pass(field, basis, up_table, 0, *outs)


def mask_words(mask, out):
    slots = mask.shape[2]
    slot = lax.broadcasted_iota(jnp.int32, (slots, WIDE), 0)

    def powers(low, high):
        value = jnp.where((slot >= low) & (slot < high), jnp.left_shift(1, slot - low), 0)
        return value.astype(F32).astype(BF16)

    for i in range(mask.shape[0]):
        row = (mask[i] != 0).astype(F32).astype(BF16)
        word = dot(row, powers(0, min(14, slots))).astype(jnp.int32)
        if slots > 14:
            word = word + jnp.left_shift(dot(row, powers(14, slots)).astype(jnp.int32), 14)
        out[i] = word


def table_kernel(packed, near_mask, mask0, mask1, mask2, table, *words):
    expand(packed, table, packed.shape[0], 6)
    for k in range(12):
        wide = table[UP_AT + k].astype(F32)
        table[DOWN_AT + k] = jnp.swapaxes(wide, 0, 1).astype(BF16)
    for mask, out in zip((near_mask, mask0, mask1, mask2), words):
        mask_words(mask, out)


def shape_of(*dims):
    return jax.ShapeDtypeStruct(tuple(dims) + (PAIRS, WIDE), BF16)


def upward_shapes(rows, cols):
    counts, _, _ = message_sizes(rows)
    edge = 2 * cols + cols + cols + cols // 2
    return [
        shape_of(rows, cols),
        shape_of(rows // 2, cols // 2),
        shape_of(rows // 4, cols // 4),
        shape_of(rows // 8, cols // 8),
        shape_of(sum(counts)),
        shape_of(sum(counts)),
        shape_of(edge),
        shape_of(edge),
    ]


VMEM = pl.BlockSpec(memory_space=pltpu.VMEM)
SMEM = pl.BlockSpec(memory_space=pltpu.SMEM)
PARAMS = pltpu.CompilerParams(vmem_limit_bytes=24 * 1024 * 1024)


def start_up(field, packed_basis, packed_up):
    rows, cols = field.shape[0], field.shape[1]
    outs = [jax.ShapeDtypeStruct((rows * cols, WIDE, WIDE), BF16)]
    outs += upward_shapes(rows, cols)
    return pl.pallas_call(
        first_kernel,
        out_shape=outs,
        in_specs=[VMEM] * 3,
        out_specs=[VMEM] * len(outs),
        scratch_shapes=[pltpu.VMEM((12, WIDE, WIDE), BF16)],
        compiler_params=PARAMS,
    )(field, packed_basis, packed_up)


def build_tables(packed, masks):
    outs = [jax.ShapeDtypeStruct((packed.shape[0] + 12, WIDE, WIDE), BF16)]
    outs += [jax.ShapeDtypeStruct(mask.shape[:2] + (WIDE,), jnp.int32) for mask in masks]
    return pl.pallas_call(
        table_kernel,
        out_shape=outs,
        in_specs=[VMEM] * 5,
        out_specs=[VMEM] * 5,
        compiler_params=PARAMS,
    )(packed, *masks)


def product(last, index, words, field, q0, q1, q2, column, received, table, basis):
    rows, cols = field.shape[0], field.shape[1]
    outs = [shape_of(rows, cols)]
    if not last:
        outs += upward_shapes(rows, cols)

    def tile_scratch(*dims):
        return pltpu.VMEM(tuple(dims) + (PAIRS, WIDE), BF16)

    args = (index, *words, field, q0, q1, q2, column, *received, table, basis)
    return pl.pallas_call(
        functools.partial(product_kernel, last, 2),
        out_shape=outs,
        in_specs=[SMEM] + [VMEM] * (len(args) - 1),
        out_specs=[VMEM] * len(outs),
        scratch_shapes=[
            tile_scratch((rows + 4) * (cols + 4)),
            tile_scratch((rows // 2 + 4) * (cols // 2 + 4)),
            tile_scratch((rows // 4 + 4) * (cols // 4 + 4)),
            tile_scratch(column.shape[0] + 1),
            tile_scratch((rows + 2) * (cols + 2)),
            tile_scratch(rows, cols),
            tile_scratch(rows // 2, cols // 2),
            tile_scratch(rows // 4, cols // 4),
            tile_scratch(rows // 8, cols // 8),
            pltpu.VMEM((rows, cols, PAIRS, WIDE), F32),
            pltpu.VMEM((1, PAIRS, SLOTS * WIDE), BF16),
        ],
        compiler_params=PARAMS,
    )(*args)


def shift(value, axis, step):
    count = lax.axis_size(axis)
    pairs = [(i, i + step) for i in range(count) if 0 <= i + step < count]
    return lax.ppermute(value, axis, pairs)


def two_by_two():
    return lax.axis_size("rhs") == 2 and lax.axis_size("sub") == 2


def exchange(rows, q3, send_l, send_r, send_u, send_d):
    counts, up, down = message_sizes(rows)
    recv_l = shift(send_r, "br", 1)
    recv_r = shift(send_l, "br", -1)
    last = down[1]
    wide = jnp.concatenate([q3[0], recv_l[last:], recv_r[last:]], 0)
    tail = []
    swap = [(0, 1), (1, 0)]
    if two_by_two():
        tail = [wide, lax.ppermute(wide, "sub", swap)]
    up_message = jnp.concatenate([send_u, recv_l[up[0] : up[1]], recv_r[up[0] : up[1]], *tail], 0)
    down_message = jnp.concatenate(
        [send_d, recv_l[down[0] : down[1]], recv_r[down[0] : down[1]], *tail], 0
    )
    recv_d = shift(up_message, ROW_AXES, -1)
    recv_u = shift(down_message, ROW_AXES, 1)
    if two_by_two():
        start = up_message.shape[0] - 2 * wide.shape[0]
        mine = jnp.where(lax.axis_index("sub") == 1, recv_d[start:], recv_u[start:])
        far = mine + lax.ppermute(mine, "sub", swap)
        column = jnp.concatenate([*tail, far], 0)
    else:
        column = lax.all_gather(wide, ROW_AXES, axis=0, tiled=True)
    return column, (recv_l, recv_r, recv_u, recv_d)


def column_place(source):
    if not two_by_two():
        return source
    rhs, sub = lax.axis_index("rhs"), lax.axis_index("sub")
    inner = source % 2
    near_place = jnp.where(inner == sub, 0, 1)
    far_place = jnp.where(inner == rhs, 2, 3)
    return jnp.where(source // 2 == rhs, near_place, far_place)


def on_device(
    sources, leaf_basis, transfer, coupling, near_table, near_mask,
    mask_leaf, mask_mid, mask_upper, mask_top,
):
    rows, cols = sources.shape[0], sources.shape[1]
    row = lax.axis_index(ROW_AXES)
    row_count = lax.axis_size(ROW_AXES)
    field = sources.reshape(rows, cols, PAIRS, WIDE)
    packed_basis = leaf_basis.reshape(rows * cols, LEAF // 2, WIDE)
    moves = transfer.reshape(12, RANK * RANK)
    packed_up = moves.reshape(12, RANK // 2, WIDE)
    basis, q0, q1, q2, q3, *sends = start_up(field, packed_basis, packed_up)
    filler = jnp.zeros((1, RANK * RANK), BF16)
    packed = jnp.concatenate([coupling.reshape(4 * 49, RANK * RANK), moves, near_table, filler], 0)
    packed = packed.reshape(DOWN_AT, RANK // 2, WIDE)
    upper = lax.dynamic_slice_in_dim(mask_upper, row * (rows // 4), rows // 4, 0)
    table, *words = build_tables(packed, (near_mask, mask_leaf, mask_mid, upper))
    index = jnp.concatenate(top_index(mask_top, row, row_count, column_place), 0)
    for step in range(PRODUCTS):
        column, received = exchange(rows, q3, *sends)
        last = step == PRODUCTS - 1
        outs = product(last, index, words, field, q0, q1, q2, column, received, table, basis)
        field = outs[0]
        if not last:
            q0, q1, q2, q3, *sends = outs[1:]
    return field.reshape(rows, cols, SIDES * LEAF)


def solution(mesh):
    placed = (
        P(("grp", "rhs", "sub"), "br", None),
        P(("grp", "rhs", "sub"), "br", None),
        P(),
        P(),
        P(),
        P(("grp", "rhs", "sub"), "br", None),
        P(("grp", "rhs", "sub"), "br", None),
        P(("grp", "rhs", "sub"), "br", None),
        P("grp", "br", None),
        P("grp", "br", None),
    )
    return jax.shard_map(
        on_device,
        mesh=mesh,
        in_specs=placed,
        out_specs=P(("grp", "rhs", "sub"), "br", None),
        check_vma=False,
    )
```

time: 199 us -> 151 us (0.76)
  Pallas kernels: 101 us -> 50.6 us
  blocking collectives: 23.7 us -> 0 us
  starting transfers between devices: 29.5 us -> 50.1 us
  waiting for transfers between devices: 9.7 us -> 17.8 us
  other arithmetic: 12.3 us -> 5.11 us
  local copies, waits for them, and re-layouts: 21.6 us -> 25.1 us
    pallas_call x3 -> x4, Pallas kernels: 96.2 us -> 45.1 us  [the longest x3 39.3 us: product(): pl.pallas_call(functools.partial(product_kernel, last, 2), out_shape=outs...]
    all_gather x3 -> x0, blocking collectives: 23.7 us -> none  [exchange(): column = lax.all_gather(wide, ROW_AXES, axis=0, tiled=True)]
    ppermute x0 -> x6, starting transfers between devices: none -> 23.2 us  [the longest x3 18.6 us: exchange(): far = mine + lax.ppermute(mine, 'sub', swap)]
    unnamed x61 -> x85, local copies, waits for them, and re-layouts: 0.3 us -> 19.2 us
    reshape x21 -> x0, local copies, waits for them, and re-layouts: 13 us -> none  [the longest x1 5.79 us: on_device(): tables = paired(coupling.reshape(4, 49, RANK, RANK))]
    concatenate x11 -> x5, other arithmetic: 11.7 us -> 3.38 us  [the longest x1 1.8 us: on_device(): jnp.concatenate([coupling.reshape(4 * 49, RANK * RANK), moves, near_table...]
    ppermute x12, waiting for transfers between devices: 9.7 us -> 14.4 us  [shift(): return lax.ppermute(value, axis, pairs)]
    squeeze x1 -> x0, local copies, waits for them, and re-layouts: 4.42 us -> none  [on_device(): tables[3]]
  transfers between devices with their start and end apart: 12 -> 18, of which waited for: 4 -> 12; matrix products, arithmetic and copies ran while one was open for 11% -> 7% of each run, Pallas kernels for 0% -> 4%
where the time goes in v2:
time: 151 us; the launch traced here: 149 us
  Pallas kernels  50.6 us (34%)
  starting transfers between devices  50.1 us (33%)
  local copies, waits for them, and re-layouts  25.1 us (17%)
  waiting for transfers between devices  17.8 us (12%)
  other arithmetic  5.11 us (3%)
    pallas_call x3, Pallas kernels, product(): pl.pallas_call(functools.partial(product_kernel, last, 2), out_shape=outs...  39.3 us
    ppermute x12, starting transfers between devices, shift(): return lax.ppermute(value, axis, pairs)  26.9 us
    unnamed x85, local copies, waits for them, and re-layouts  19.2 us
    ppermute x3, starting transfers between devices, exchange(): far = mine + lax.ppermute(mine, 'sub', swap)  18.6 us
    ppermute x12, waiting for transfers between devices, shift(): return lax.ppermute(value, axis, pairs)  14.4 us
    pallas_call x1, Pallas kernels, build_tables(): pl.pallas_call(table_kernel, out_shape=outs, in_specs=[VMEM] * 5, out_spe...  5.81 us
    pallas_call x1, Pallas kernels, start_up(): pl.pallas_call(first_kernel, out_shape=outs, in_specs=[VMEM] * 3, out_spe...  5.53 us
    ppermute x3, starting transfers between devices, exchange(): tail = [wide, lax.ppermute(wide, 'sub', swap)]  4.6 us
  transfers between devices with their start and end apart: 18, of which 12 were waited for; matrix products, arithmetic and copies ran while one was open for 7% of the time, Pallas kernels for 4%

profile of v2, /device:TPU:15, one launch (start us, length us, event | category | flops | bytes accessed | tf_op | source)
XLA Modules:
  0.0 149.3 jit_solution(15520444166214851874)
XLA Ops:
  2.6 5.5 %shard_map.209 = (bf16[128,128,128]{2,1,0:T(8,128)(2,1)S(1)}, bf16[8,16,16,128]{3,2,1,0:T(8,128)(2,1)S(1)}, bf16[4,8,16,128]{3,2,1,0:T(8,128)(2,1)S(1)}, bf16[2,...) custom-call(bf16[8,16,16,128]{3,2,1,0:T(8,128)(2,1)S(1)} %bitcast.37, ...), custom_call_target="tpu_custom_call" | custom-call | tf_op jit(solution)/shard_map/pallas_call | solution.py:408
  8.2 2.0 %copy-done.1 = bf16[128,128,128]{2,1,0:T(8,128)(2,1)} copy-done((bf16[128,128,128]{2,1,0:T(8,128)(2,1)}, bf16[128,128,128]{2,1,0:T(8,128)(2,1)S(1)}, u32[]{:S(2)}) %copy-start.1) | copy-done | bytes 4194328
  12.2 3.2 %collective-permute-start = (bf16[38,16,128]{2,1,0:T(8,128)(2,1)S(1)}, bf16[38,16,128]{2,1,0:T(8,128)(2,1)S(1)}, u32[]{:S(2)}, u32[]{:S(2)}) collective-permute-start(bf16[38,16,128]{2,1,0:T(8,128)(2,1)S(1)} %get-tuple-element.45), channel_id=1, source_target_pairs={{0,4},{4,8},{8,12},{1,5},{5,9},{9,13},{2,6},{6,10},{10,14},{3,7},{... | collective-permute-start | bytes 466952 | tf_op jit(solution)/shard_map/ppermute | solution.py:465
  15.4 2.1 %collective-permute-start.1 = (bf16[38,16,128]{2,1,0:T(8,128)(2,1)S(1)}, bf16[38,16,128]{2,1,0:T(8,128)(2,1)S(1)}, u32[]{:S(2)}, u32[]{:S(2)}) collective-permute-start(bf16[38,16,128]{2,1,0:T(8,128)(2,1)S(1)} %get-tuple-element.46), channel_id=1, source_target_pairs={{4,0},{8,4},{12,8},{5,1},{9,5},{13,9},{6,2},{10,6},{14,10},{7,3},{... | collective-permute-start | bytes 466952 | tf_op jit(solution)/shard_map/ppermute | solution.py:465
  27.0 2.3 %copy.25 = bf16[4,49,4096]{2,1,0:T(8,128)(2,1)S(1)} copy(bf16[4,49,4096]{2,0,1:T(4,128)(2,1)} %param.25) | data formatting | bytes 3211264 | tf_op args[3]
  32.4 2.0 %collective-permute-start.3 = (bf16[110,16,128]{2,1,0:T(8,128)(2,1)}, bf16[110,16,128]{2,1,0:T(8,128)(2,1)S(1)}, u32[]{:S(2)}, u32[]{:S(2)}) collective-permute-start(bf16[110,16,128]{2,1,0:T(8,128)(2,1)} %get-tuple-element.113), channel_id=1, source_target_pairs={{1,0},{2,1},{3,2},{5,4},{6,5},{7,6},{9,8},{10,9},{11,10},{13,12},{... | collective-permute-start | bytes 1351688 | tf_op jit(solution)/shard_map/ppermute | solution.py:465
  39.0 6.5 %collective-permute-start.5 = (bf16[12,16,128]{2,1,0:T(8,128)(2,1)}, bf16[12,16,128]{2,1,0:T(8,128)(2,1)}, u32[]{:S(2)}, u32[]{:S(2)}) collective-permute-start(bf16[12,16,128]{2,1,0:T(8,128)(2,1)} %slice_select_fusion.2), channel_id=1, source_target_pairs={{0,1},{1,0},{2,3},{3,2},{4,5},{5,4},{6,7},{7,6},{8,9},{9,8},{10,11... | collective-permute-start | bytes 147464 | tf_op jit(solution)/shard_map/ppermute | solution.py:491
  47.2 5.8 %shard_map.208 = (bf16[230,128,128]{2,1,0:T(8,128)(2,1)S(1)}, s32[8,16,128]{2,1,0:T(8,128)S(1)}, s32[8,16,128]{2,1,0:T(8,128)S(1)}, s32[4,8,128]{2,1,0:T(8,128)S(1)}, s32[2,4,128]{2,1,0:T(4,128)S(1)}) custom-call(bf16[218,32,128]{2,1,0:T(8,128)(2,1)S(1)} %maximum_maximum_fusion.packed, s32[8,16,9]{2,1,0:T(8,128)S(1)} %copy.26.near_mask, ...), custom_call_target="tpu_custom_call" | custom-call | tf_op jit(solution)/shard_map/pallas_call | solution.py:421
  54.5 2.2 %copy-done.2 = bf16[128,128,128]{2,1,0:T(8,128)(2,1)S(1)} copy-done((bf16[128,128,128]{2,1,0:T(8,128)(2,1)S(1)}, bf16[128,128,128]{2,1,0:T(8,128)(2,1)}, u32[]{:S(2)}) %copy-start.2) | copy-done | bytes 4194328
  59.2 14.0 %shard_map.210 = (bf16[8,16,16,128]{3,2,1,0:T(8,128)(2,1)S(1)}, bf16[8,16,16,128]{3,2,1,0:T(8,128)(2,1)S(1)}, bf16[4,8,16,128]{3,2,1,0:T(8,128)(2,1)S(1)}, bf16[...) custom-call(s32[108]{0:T(128)S(1)} %pad_add_fusion.refs_0_, ...), custom_call_target="tpu_custom_call" | custom-call | tf_op jit(solution)/shard_map/pallas_call | solution.py:440
  73.2 3.2 %collective-permute-start.6 = (bf16[38,16,128]{2,1,0:T(8,128)(2,1)S(1)}, bf16[38,16,128]{2,1,0:T(8,128)(2,1)S(1)}, u32[]{:S(2)}, u32[]{:S(2)}) collective-permute-start(bf16[38,16,128]{2,1,0:T(8,128)(2,1)S(1)} %get-tuple-element.56), channel_id=1, source_target_pairs={{0,4},{4,8},{8,12},{1,5},{5,9},{9,13},{2,6},{6,10},{10,14},{3,7},{... | collective-permute-start | bytes 466952 | tf_op jit(solution)/shard_map/ppermute | solution.py:465
  76.4 2.1 %collective-permute-start.7 = (bf16[38,16,128]{2,1,0:T(8,128)(2,1)S(1)}, bf16[38,16,128]{2,1,0:T(8,128)(2,1)S(1)}, u32[]{:S(2)}, u32[]{:S(2)}) collective-permute-start(bf16[38,16,128]{2,1,0:T(8,128)(2,1)S(1)} %get-tuple-element.57), channel_id=1, source_target_pairs={{4,0},{8,4},{12,8},{5,1},{9,5},{13,9},{6,2},{10,6},{14,10},{7,3},{... | collective-permute-start | bytes 466952 | tf_op jit(solution)/shard_map/ppermute | solution.py:465
  78.6 2.2 %collective-permute-done.6.refs_10_ = bf16[38,16,128]{2,1,0:T(8,128)(2,1)S(1)} collective-permute-done((bf16[38,16,128]{2,1,0:T(8,128)(2,1)S(1)}, bf16[38,16,128]{2,1,0:T(8,128)(2,1)S(1)}, u32[]{:S(2)}, u32[]{:S(2)}) %collective-permute-start.6) | collective-permute-done | bytes 155680 | tf_op jit(solution)/shard_map/ppermute | solution.py:465
  80.8 2.9 %collective-permute-done.7.refs_11_ = bf16[38,16,128]{2,1,0:T(8,128)(2,1)S(1)} collective-permute-done((bf16[38,16,128]{2,1,0:T(8,128)(2,1)S(1)}, bf16[38,16,128]{2,1,0:T(8,128)(2,1)S(1)}, u32[]{:S(2)}, u32[]{:S(2)}) %collective-permute-start.7) | collective-permute-done | bytes 155680 | tf_op jit(solution)/shard_map/ppermute | solution.py:465
  85.8 2.3 %collective-permute-start.9 = (bf16[110,16,128]{2,1,0:T(8,128)(2,1)S(1)}, bf16[110,16,128]{2,1,0:T(8,128)(2,1)S(1)}, u32[]{:S(2)}, u32[]{:S(2)}) collective-permute-start(bf16[110,16,128]{2,1,0:T(8,128)(2,1)S(1)} %get-tuple-element.110), channel_id=1, source_target_pairs={{1,0},{2,1},{3,2},{5,4},{6,5},{7,6},{9,8},{10,9},{11,10},{13,12},{... | collective-permute-start | bytes 1351688 | tf_op jit(solution)/shard_map/ppermute | solution.py:465
  89.6 2.2 %collective-permute-done.10.refs_12_ = bf16[110,16,128]{2,1,0:T(8,128)(2,1)S(1)} collective-permute-done((bf16[110,16,128]{2,1,0:T(8,128)(2,1)S(1)}, bf16[110,16,128]{2,1,0:T(8,128)(2,1)S(1)}, u32[]{:S(2)}, u32[]{:S(2)}) %collective-permute-start.10) | collective-permute-done | bytes 450592 | tf_op jit(solution)/shard_map/ppermute | solution.py:465
  91.8 6.1 %collective-permute-start.11 = (bf16[12,16,128]{2,1,0:T(8,128)(2,1)S(1)}, bf16[12,16,128]{2,1,0:T(8,128)(2,1)S(1)}, u32[]{:S(2)}, u32[]{:S(2)}) collective-permute-start(bf16[12,16,128]{2,1,0:T(8,128)(2,1)S(1)} %slice_select_fusion.1), channel_id=1, source_target_pairs={{0,1},{1,0},{2,3},{3,2},{4,5},{5,4},{6,7},{7,6},{8,9},{9,8},{10,11... | collective-permute-start | bytes 147464 | tf_op jit(solution)/shard_map/ppermute | solution.py:491
  98.7 14.0 %shard_map.211 = (bf16[8,16,16,128]{3,2,1,0:T(8,128)(2,1)S(1)}, bf16[8,16,16,128]{3,2,1,0:T(8,128)(2,1)S(1)}, bf16[4,8,16,128]{3,2,1,0:T(8,128)(2,1)S(1)}, bf16[...) custom-call(s32[108]{0:T(128)S(1)} %pad_add_fusion.refs_0_, ...), custom_call_target="tpu_custom_call" | custom-call | tf_op jit(solution)/shard_map/pallas_call | solution.py:440
  112.8 1.9 %collective-permute-start.12 = (bf16[38,16,128]{2,1,0:T(8,128)(2,1)S(1)}, bf16[38,16,128]{2,1,0:T(8,128)(2,1)S(1)}, u32[]{:S(2)}, u32[]{:S(2)}) collective-permute-start(bf16[38,16,128]{2,1,0:T(8,128)(2,1)S(1)} %get-tuple-element.65), channel_id=1, source_target_pairs={{0,4},{4,8},{8,12},{1,5},{5,9},{9,13},{2,6},{6,10},{10,14},{3,7},{... | collective-permute-start | bytes 466952 | tf_op jit(solution)/shard_map/ppermute | solution.py:465
  114.7 3.4 %collective-permute-start.13 = (bf16[38,16,128]{2,1,0:T(8,128)(2,1)S(1)}, bf16[38,16,128]{2,1,0:T(8,128)(2,1)S(1)}, u32[]{:S(2)}, u32[]{:S(2)}) collective-permute-start(bf16[38,16,128]{2,1,0:T(8,128)(2,1)S(1)} %get-tuple-element.66), channel_id=1, source_target_pairs={{4,0},{8,4},{12,8},{5,1},{9,5},{13,9},{6,2},{10,6},{14,10},{7,3},{... | collective-permute-start | bytes 466952 | tf_op jit(solution)/shard_map/ppermute | solution.py:465
  124.1 2.3 %collective-permute-start.15 = (bf16[110,16,128]{2,1,0:T(8,128)(2,1)S(1)}, bf16[110,16,128]{2,1,0:T(8,128)(2,1)S(1)}, u32[]{:S(2)}, u32[]{:S(2)}) collective-permute-start(bf16[110,16,128]{2,1,0:T(8,128)(2,1)S(1)} %get-tuple-element.107), channel_id=1, source_target_pairs={{1,0},{2,1},{3,2},{5,4},{6,5},{7,6},{9,8},{10,9},{11,10},{13,12},{... | collective-permute-start | bytes 1351688 | tf_op jit(solution)/shard_map/ppermute | solution.py:465
  127.9 2.1 %collective-permute-done.16.refs_12_ = bf16[110,16,128]{2,1,0:T(8,128)(2,1)S(1)} collective-permute-done((bf16[110,16,128]{2,1,0:T(8,128)(2,1)S(1)}, bf16[110,16,128]{2,1,0:T(8,128)(2,1)S(1)}, u32[]{:S(2)}, u32[]{:S(2)}) %collective-permute-start.16) | collective-permute-done | bytes 450592 | tf_op jit(solution)/shard_map/ppermute | solution.py:465
  130.1 6.1 %collective-permute-start.17 = (bf16[12,16,128]{2,1,0:T(8,128)(2,1)S(1)}, bf16[12,16,128]{2,1,0:T(8,128)(2,1)S(1)}, u32[]{:S(2)}, u32[]{:S(2)}) collective-permute-start(bf16[12,16,128]{2,1,0:T(8,128)(2,1)S(1)} %slice_select_fusion), channel_id=1, source_target_pairs={{0,1},{1,0},{2,3},{3,2},{4,5},{5,4},{6,7},{7,6},{8,9},{9,8},{10,11... | collective-permute-start | bytes 147464 | tf_op jit(solution)/shard_map/ppermute | solution.py:491
  137.0 11.3 %shard_map.212 = bf16[8,16,16,128]{3,2,1,0:T(8,128)(2,1)S(1)} custom-call(s32[108]{0:T(128)S(1)} %pad_add_fusion.refs_0_, s32[8,16,128]{2,1,0:T(8,128)S(1)} %get-tuple-element.37.refs_1_, s32[8,16,128]{2,1,0:T(8,128)S(1)} %get-tuple-element.38.refs_2_, s32[4,8,128]{2,1,0:T(8,128)S(1)} %get-tuple-element.39.refs_3_, ...), custom_call_target="tpu_custom_call" | custom-call | tf_op jit(solution)/shard_map/pallas_call | solution.py:440
  (126 shorter events, 41.4 us)
Async XLA Ops:
  0.0 26.3 %copy-start = (s32[8,4,27]{2,1,0:T(4,128)S(1)}, s32[8,4,27]{2,1,0:T(4,128)}, u32[]{:S(2)}) copy-start(s32[8,4,27]{2,1,0:T(4,128)} %param.30) | copy-start | bytes 10372
  2.3 16.4 %copy-start.22 = (s32[27]{0:T(128)S(1)}, s32[27]{0:T(128)}, u32[]{:S(2)}) copy-start(s32[27]{0:T(128)} %constant.97.clone) | copy-start | bytes 328
  2.3 16.4 %copy-start.23 = (s32[27]{0:T(128)S(1)}, s32[27]{0:T(128)}, u32[]{:S(2)}) copy-start(s32[27]{0:T(128)} %constant.96.clone) | copy-start | bytes 328
  2.3 16.4 %copy-start.24 = (s32[27]{0:T(128)S(1)}, s32[27]{0:T(128)}, u32[]{:S(2)}) copy-start(s32[27]{0:T(128)} %constant.95.clone) | copy-start | bytes 328
  2.6 23.7 %copy-start.17 = (bf16[9,4096]{1,0:T(8,128)(2,1)S(1)}, bf16[9,4096]{1,0:T(8,128)(2,1)}, u32[]{:S(2)}) copy-start(bf16[9,4096]{1,0:T(8,128)(2,1)} %param.26) | copy-start | bytes 221188
  12.2 8.0 %collective-permute-start = (bf16[38,16,128]{2,1,0:T(8,128)(2,1)S(1)}, bf16[38,16,128]{2,1,0:T(8,128)(2,1)S(1)}, u32[]{:S(2)}, u32[]{:S(2)}) collective-permute-start(bf16[38,16,128]{2,1,0:T(8,128)(2,1)S(1)} %get-tuple-element.45), channel_id=1, source_target_pairs={{0,4},{4,8},{8,12},{1,5},{5,9},{9,13},{2,6},{6,10},{10,14},{3,7},{... | collective-permute-start | bytes 466952 | tf_op jit(solution)/shard_map/ppermute | solution.py:465
  15.4 6.5 %collective-permute-start.1 = (bf16[38,16,128]{2,1,0:T(8,128)(2,1)S(1)}, bf16[38,16,128]{2,1,0:T(8,128)(2,1)S(1)}, u32[]{:S(2)}, u32[]{:S(2)}) collective-permute-start(bf16[38,16,128]{2,1,0:T(8,128)(2,1)S(1)} %get-tuple-element.46), channel_id=1, source_target_pairs={{4,0},{8,4},{12,8},{5,1},{9,5},{13,9},{6,2},{10,6},{14,10},{7,3},{... | collective-permute-start | bytes 466952 | tf_op jit(solution)/shard_map/ppermute | solution.py:465
  24.4 6.7 %collective-permute-start.2 = (bf16[6,16,128]{2,1,0:T(8,128)(2,1)S(1)}, bf16[6,16,128]{2,1,0:T(8,128)(2,1)S(1)}, u32[]{:S(2)}, u32[]{:S(2)}) collective-permute-start(bf16[6,16,128]{2,1,0:T(8,128)(2,1)S(1)} %pad_maximum_fusion), channel_id=1, source_target_pairs={{0,1},{1,0},{2,3},{3,2},{4,5},{5,4},{6,7},{7,6},{8,9},{9,8},{10,11... | collective-permute-start | bytes 73736 | tf_op jit(solution)/shard_map/ppermute | solution.py:481
  32.4 5.3 %collective-permute-start.3 = (bf16[110,16,128]{2,1,0:T(8,128)(2,1)}, bf16[110,16,128]{2,1,0:T(8,128)(2,1)S(1)}, u32[]{:S(2)}, u32[]{:S(2)}) collective-permute-start(bf16[110,16,128]{2,1,0:T(8,128)(2,1)} %get-tuple-element.113), channel_id=1, source_target_pairs={{1,0},{2,1},{3,2},{5,4},{6,5},{7,6},{9,8},{10,9},{11,10},{13,12},{... | collective-permute-start | bytes 1351688 | tf_op jit(solution)/shard_map/ppermute | solution.py:465
  34.3 4.0 %collective-permute-start.4 = (bf16[110,16,128]{2,1,0:T(8,128)(2,1)}, bf16[110,16,128]{2,1,0:T(8,128)(2,1)S(1)}, u32[]{:S(2)}, u32[]{:S(2)}) collective-permute-start(bf16[110,16,128]{2,1,0:T(8,128)(2,1)} %get-tuple-element.115), channel_id=1, source_target_pairs={{0,1},{1,2},{2,3},{4,5},{5,6},{6,7},{8,9},{9,10},{10,11},{12,13},{... | collective-permute-start | bytes 1351688 | tf_op jit(solution)/shard_map/ppermute | solution.py:465
  39.0 14.0 %collective-permute-start.5 = (bf16[12,16,128]{2,1,0:T(8,128)(2,1)}, bf16[12,16,128]{2,1,0:T(8,128)(2,1)}, u32[]{:S(2)}, u32[]{:S(2)}) collective-permute-start(bf16[12,16,128]{2,1,0:T(8,128)(2,1)} %slice_select_fusion.2), channel_id=1, source_target_pairs={{0,1},{1,0},{2,3},{3,2},{4,5},{5,4},{6,7},{7,6},{8,9},{9,8},{10,11... | collective-permute-start | bytes 147464 | tf_op jit(solution)/shard_map/ppermute | solution.py:491
  59.2 39.5 %copy-start.3 = (bf16[128,128,128]{2,1,0:T(8,128)(2,1)S(1)}, bf16[128,128,128]{2,1,0:T(8,128)(2,1)}, u32[]{:S(2)}) copy-start(bf16[128,128,128]{2,1,0:T(8,128)(2,1)} %copy-done.1) | copy-start | bytes 12582916
  73.2 7.5 %collective-permute-start.6 = (bf16[38,16,128]{2,1,0:T(8,128)(2,1)S(1)}, bf16[38,16,128]{2,1,0:T(8,128)(2,1)S(1)}, u32[]{:S(2)}, u32[]{:S(2)}) collective-permute-start(bf16[38,16,128]{2,1,0:T(8,128)(2,1)S(1)} %get-tuple-element.56), channel_id=1, source_target_pairs={{0,4},{4,8},{8,12},{1,5},{5,9},{9,13},{2,6},{6,10},{10,14},{3,7},{... | collective-permute-start | bytes 466952 | tf_op jit(solution)/shard_map/ppermute | solution.py:465
  76.4 7.2 %collective-permute-start.7 = (bf16[38,16,128]{2,1,0:T(8,128)(2,1)S(1)}, bf16[38,16,128]{2,1,0:T(8,128)(2,1)S(1)}, u32[]{:S(2)}, u32[]{:S(2)}) collective-permute-start(bf16[38,16,128]{2,1,0:T(8,128)(2,1)S(1)} %get-tuple-element.57), channel_id=1, source_target_pairs={{4,0},{8,4},{12,8},{5,1},{9,5},{13,9},{6,2},{10,6},{14,10},{7,3},{... | collective-permute-start | bytes 466952 | tf_op jit(solution)/shard_map/ppermute | solution.py:465
  83.7 2.0 %collective-permute-start.8 = (bf16[6,16,128]{2,1,0:T(8,128)(2,1)S(1)}, bf16[6,16,128]{2,1,0:T(8,128)(2,1)S(1)}, u32[]{:S(2)}, u32[]{:S(2)}) collective-permute-start(bf16[6,16,128]{2,1,0:T(8,128)(2,1)S(1)} %pad_maximum_fusion.1), channel_id=1, source_target_pairs={{0,1},{1,0},{2,3},{3,2},{4,5},{5,4},{6,7},{7,6},{8,9},{9,8},{10,11... | collective-permute-start | bytes 73736 | tf_op jit(solution)/shard_map/ppermute | solution.py:481
  85.8 3.8 %collective-permute-start.9 = (bf16[110,16,128]{2,1,0:T(8,128)(2,1)S(1)}, bf16[110,16,128]{2,1,0:T(8,128)(2,1)S(1)}, u32[]{:S(2)}, u32[]{:S(2)}) collective-permute-start(bf16[110,16,128]{2,1,0:T(8,128)(2,1)S(1)} %get-tuple-element.110), channel_id=1, source_target_pairs={{1,0},{2,1},{3,2},{5,4},{6,5},{7,6},{9,8},{10,9},{11,10},{13,12},{... | collective-permute-start | bytes 1351688 | tf_op jit(solution)/shard_map/ppermute | solution.py:465
  88.1 3.7 %collective-permute-start.10 = (bf16[110,16,128]{2,1,0:T(8,128)(2,1)S(1)}, bf16[110,16,128]{2,1,0:T(8,128)(2,1)S(1)}, u32[]{:S(2)}, u32[]{:S(2)}) collective-permute-start(bf16[110,16,128]{2,1,0:T(8,128)(2,1)S(1)} %get-tuple-element.112), channel_id=1, source_target_pairs={{0,1},{1,2},{2,3},{4,5},{5,6},{6,7},{8,9},{9,10},{10,11},{12,13},{... | collective-permute-start | bytes 1351688 | tf_op jit(solution)/shard_map/ppermute | solution.py:465
  91.8 6.9 %collective-permute-start.11 = (bf16[12,16,128]{2,1,0:T(8,128)(2,1)S(1)}, bf16[12,16,128]{2,1,0:T(8,128)(2,1)S(1)}, u32[]{:S(2)}, u32[]{:S(2)}) collective-permute-start(bf16[12,16,128]{2,1,0:T(8,128)(2,1)S(1)} %slice_select_fusion.1), channel_id=1, source_target_pairs={{0,1},{1,0},{2,3},{3,2},{4,5},{5,4},{6,7},{7,6},{8,9},{9,8},{10,11... | collective-permute-start | bytes 147464 | tf_op jit(solution)/shard_map/ppermute | solution.py:491
  112.8 7.1 %collective-permute-start.12 = (bf16[38,16,128]{2,1,0:T(8,128)(2,1)S(1)}, bf16[38,16,128]{2,1,0:T(8,128)(2,1)S(1)}, u32[]{:S(2)}, u32[]{:S(2)}) collective-permute-start(bf16[38,16,128]{2,1,0:T(8,128)(2,1)S(1)} %get-tuple-element.65), channel_id=1, source_target_pairs={{0,4},{4,8},{8,12},{1,5},{5,9},{9,13},{2,6},{6,10},{10,14},{3,7},{... | collective-permute-start | bytes 466952 | tf_op jit(solution)/shard_map/ppermute | solution.py:465
  114.7 6.8 %collective-permute-start.13 = (bf16[38,16,128]{2,1,0:T(8,128)(2,1)S(1)}, bf16[38,16,128]{2,1,0:T(8,128)(2,1)S(1)}, u32[]{:S(2)}, u32[]{:S(2)}) collective-permute-start(bf16[38,16,128]{2,1,0:T(8,128)(2,1)S(1)} %get-tuple-element.66), channel_id=1, source_target_pairs={{4,0},{8,4},{12,8},{5,1},{9,5},{13,9},{6,2},{10,6},{14,10},{7,3},{... | collective-permute-start | bytes 466952 | tf_op jit(solution)/shard_map/ppermute | solution.py:465
  121.6 2.4 %collective-permute-start.14 = (bf16[6,16,128]{2,1,0:T(8,128)(2,1)S(1)}, bf16[6,16,128]{2,1,0:T(8,128)(2,1)S(1)}, u32[]{:S(2)}, u32[]{:S(2)}) collective-permute-start(bf16[6,16,128]{2,1,0:T(8,128)(2,1)S(1)} %pad_maximum_fusion.2), channel_id=1, source_target_pairs={{0,1},{1,0},{2,3},{3,2},{4,5},{5,4},{6,7},{7,6},{8,9},{9,8},{10,11... | collective-permute-start | bytes 73736 | tf_op jit(solution)/shard_map/ppermute | solution.py:481
  124.1 3.8 %collective-permute-start.15 = (bf16[110,16,128]{2,1,0:T(8,128)(2,1)S(1)}, bf16[110,16,128]{2,1,0:T(8,128)(2,1)S(1)}, u32[]{:S(2)}, u32[]{:S(2)}) collective-permute-start(bf16[110,16,128]{2,1,0:T(8,128)(2,1)S(1)} %get-tuple-element.107), channel_id=1, source_target_pairs={{1,0},{2,1},{3,2},{5,4},{6,5},{7,6},{9,8},{10,9},{11,10},{13,12},{... | collective-permute-start | bytes 1351688 | tf_op jit(solution)/shard_map/ppermute | solution.py:465
  126.3 3.7 %collective-permute-start.16 = (bf16[110,16,128]{2,1,0:T(8,128)(2,1)S(1)}, bf16[110,16,128]{2,1,0:T(8,128)(2,1)S(1)}, u32[]{:S(2)}, u32[]{:S(2)}) collective-permute-start(bf16[110,16,128]{2,1,0:T(8,128)(2,1)S(1)} %get-tuple-element.109), channel_id=1, source_target_pairs={{0,1},{1,2},{2,3},{4,5},{5,6},{6,7},{8,9},{9,10},{10,11},{12,13},{... | collective-permute-start | bytes 1351688 | tf_op jit(solution)/shard_map/ppermute | solution.py:465
  130.1 6.9 %collective-permute-start.17 = (bf16[12,16,128]{2,1,0:T(8,128)(2,1)S(1)}, bf16[12,16,128]{2,1,0:T(8,128)(2,1)S(1)}, u32[]{:S(2)}, u32[]{:S(2)}) collective-permute-start(bf16[12,16,128]{2,1,0:T(8,128)(2,1)S(1)} %slice_select_fusion), channel_id=1, source_target_pairs={{0,1},{1,0},{2,3},{3,2},{4,5},{5,4},{6,7},{7,6},{8,9},{9,8},{10,11... | collective-permute-start | bytes 147464 | tf_op jit(solution)/shard_map/ppermute | solution.py:491
  (24 other events, 157.3 us)
